TPU v7x, 512 devices: a whole 4x8x8 slice. The times are simulated.
512 devices in a mesh: frames: 32 (over x, y_lo, core), labels: 16 (over z, y_hi).
Axes of the slice: x: 4, y: 8 (y_hi: 2, y_lo: 4; y = y_hi * 4 + y_lo), z: 8, core: 2. Of those that a mesh axis runs over, the one named last changes fastest.
Arguments:
- encoder_out: bfloat16 [3072, 640], P('frames'), may hold values from -6 to 6
- predictor_out: bfloat16 [256, 640], P('labels'), may hold values from -6 to 6
- out_weight: bfloat16 [640, 1024], replicated, may hold values from -0.25 to 0.25
- out_bias: float32 [1024], replicated, may hold values from -4 to 4
- target_labels: int32 [256], P('labels'), may hold values from 1 to 1023
- lengths: int32 [2], replicated, may hold values from 1 to 3072, as said below
- alpha_saved: float32 [3072, 256], P('frames', 'labels')
- beta_saved: float32 [3072, 256], P('frames', 'labels')
- log_likelihood: float32 [1], replicated, may hold values from -839.5 to -838.5
Outputs:
- grad_encoder: float32 [3072, 640], P('frames', 'labels')
- grad_predictor: float32 [256, 640], P('labels', 'frames')
- grad_weight: float32 [640, 1024], replicated
- grad_bias: float32 [1024], replicated
Inputs may be any that keep to these rules, and one draw needn't show every extreme that they name: `lengths`: the frame length is 3072 and the label length lies in 240 to 255.
All inputs are finite; a program needn't handle non-finite values.
Results may differ from a plain program's by a relative error of at most 0.0034.
Values sent between devices are 32-bit elements; how exact they have to be, the bound alone decides.
A program may use at most 64 MiB of HBM per device.

v0:
```python
import jax
import jax.numpy as jnp
from jax import lax
from jax.sharding import PartitionSpec as P


def from_behind(array, axis, by):
    length = lax.axis_size(axis)
    pairs = [(i, i + by) for i in range(length) if 0 <= i + by < length]
    return lax.ppermute(array, axis, pairs)


def local(
    encoder_out,
    predictor_out,
    out_weight,
    out_bias,
    target_labels,
    lengths,
    alpha_saved,
    beta_saved,
    log_likelihood,
):
    frame_rows = encoder_out.shape[0]
    label_cols = predictor_out.shape[0]
    width = out_weight.shape[0]
    vocab = out_weight.shape[1]
    frame_len = lengths[0]
    label_len = lengths[1]
    log_total = log_likelihood[0]
    next_row = from_behind(beta_saved[0:1, :], "frames", -1)
    next_col = from_behind(beta_saved[:, 0:1], "labels", -1)
    beta_frame = jnp.concatenate([beta_saved[1:], next_row], axis=0)
    beta_label = jnp.concatenate([beta_saved[:, 1:], next_col], axis=1)
    vocab_ids = jnp.arange(vocab, dtype=jnp.int32)
    label_hot = (target_labels[:, None] == vocab_ids[None, :]).astype(jnp.float32)
    blank_hot = (vocab_ids == 0).astype(jnp.float32)
    frame_pos = (
        lax.axis_index("frames") * frame_rows + jnp.arange(frame_rows, dtype=jnp.int32)[:, None]
    )
    label_pos = (
        lax.axis_index("labels") * label_cols + jnp.arange(label_cols, dtype=jnp.int32)[None, :]
    )
    joint = jnp.tanh(
        encoder_out.astype(jnp.float32)[:, None, :] + predictor_out.astype(jnp.float32)[None, :, :]
    )
    joint = joint.astype(jnp.bfloat16).reshape(frame_rows * label_cols, width)
    logits = jnp.dot(joint, out_weight, preferred_element_type=jnp.float32) + out_bias[None, :]
    lse = jnp.log(jnp.sum(jnp.exp(logits), axis=-1))
    probs = jnp.exp(logits - lse[:, None]).reshape(frame_rows, label_cols, vocab)
    logits3 = logits.reshape(frame_rows, label_cols, vocab)
    lse2 = lse.reshape(frame_rows, label_cols)
    lp_blank = logits3[:, :, 0] - lse2
    lp_label = jnp.sum(logits3 * label_hot[None, :, :], axis=-1) - lse2
    inner = (frame_pos < frame_len - 1) & (label_pos <= label_len)
    final = (frame_pos == frame_len - 1) & (label_pos == label_len)
    blank_ok = inner | final
    blank_arg = alpha_saved + lp_blank + jnp.where(inner, beta_frame, 0.0) - log_total
    blank_occ = jnp.where(blank_ok, jnp.exp(jnp.where(blank_ok, blank_arg, 0.0)), 0.0)
    label_ok = (frame_pos < frame_len) & (label_pos < label_len)
    label_arg = alpha_saved + lp_label + beta_label - log_total
    label_occ = jnp.where(label_ok, jnp.exp(jnp.where(label_ok, label_arg, 0.0)), 0.0)
    grad_logits = (
        (
            (blank_occ + label_occ)[:, :, None] * probs
            - blank_occ[:, :, None] * blank_hot[None, None, :]
            - label_occ[:, :, None] * label_hot[None, :, :]
        )
        .astype(jnp.bfloat16)
        .reshape(frame_rows * label_cols, vocab)
    )
    grad_joint = lax.dot_general(
        grad_logits, out_weight, (((1,), (1,)), ((), ())), preferred_element_type=jnp.float32
    )
    joint_f = joint.astype(jnp.float32)
    grad_pre = (grad_joint * (1.0 - joint_f * joint_f)).reshape(frame_rows, label_cols, width)
    enc_term = jnp.sum(grad_pre, axis=1)
    pred_term = jnp.sum(grad_pre, axis=0)
    weight_term = lax.dot_general(
        joint, grad_logits, (((0,), (0,)), ((), ())), preferred_element_type=jnp.float32
    )
    bias_term = jnp.sum(grad_logits.astype(jnp.float32), axis=0)
    grad_encoder = lax.psum_scatter(enc_term, "labels", scatter_dimension=1, tiled=True)
    grad_predictor = lax.psum_scatter(pred_term, "frames", scatter_dimension=1, tiled=True)
    grad_weight, grad_bias = lax.psum((weight_term, bias_term), ("frames", "labels"))
    return (grad_encoder, grad_predictor, grad_weight, grad_bias)


def solution(mesh):
    placed = (
        P("frames", None),
        P("labels", None),
        P(),
        P(),
        P("labels"),
        P(),
        P("frames", "labels"),
        P("frames", "labels"),
        P(),
    )
    return jax.shard_map(
        local,
        mesh=mesh,
        in_specs=placed,
        out_specs=(P("frames", "labels"), P("labels", "frames"), P(), P()),
        check_vma=False,
    )
```

profile of v0, /device:TPU:1, one launch (start us, length us, event | category | flops | bytes accessed | tf_op | source)
XLA Modules:
  0.0 373.4 jit_solution(1014637734543184065)
XLA Ops:
  8.0 0.0 reduce-scatter.5.cloned.1.call-start
  8.1 1.3 slice.27
  9.4 1.3 collective-permute-start.1
  10.7 8.8 %collective-permute-start = (f32[1,16]{0,1:T(8,128)}, f32[1,16]{0,1:T(8,128)}, u32[]{:S(2)}, u32[]{:S(2)}) collective-permute-start(f32[1,16]{0,1:T(8,128)} %bitcast.41), channel_id=1, source_target_pairs={{16,0},{32,16},{48,32},{64,48},{80,64},{96,80},{112,96},{128,112},... | collective-permute-start | bytes 200 | tf_op jit(solution)/shard_map/ppermute | solution.py:10
  19.5 1.3 fusion.35
  20.8 1.2 fusion.27
  22.0 1.2 fusion.25
  23.1 0.6 fusion.24
  23.7 0.8 slice.24
  24.5 0.7 slice.26
  26.5 1.2 fusion.28
  27.7 0.6 fusion.29
  28.3 0.7 convert_element_type.42
  29.0 1.4 copy.32
  30.4 0.7 fusion.16
  31.2 0.9 convert_element_type.41
  32.1 0.6 tanh_convert_fusion
  32.7 0.6 copy.30
  33.4 5.4 %fusion = (f32[1536]{0:T(1024)S(1)}, f32[1536]{0:T(1024)S(1)}, f32[1536,1024]{1,0:T(8,128)}) fusion(f32[16,1024]{1,0:T(8,128)S(1)} %fusion.16, f32[1024]{0:T(1024)S(1)} %copy-done.10, bf16[1536,640]{1,0:T(8,128)(2,1)S(1)} %bitcast.37, bf16[640,1024]{1,0:T(8,128)(2,1)S(1)} %copy-done), kind=kOutput, calls=%fused_computation.2 | convolution fusion | flops 2019554304 | bytes 9650176 | tf_op jit(solution)/shard_map/dot_general | solution.py:48
  38.8 0.7 reduce_sum.49
  39.5 0.7 log.12
  40.2 2.1 slice.28
  42.3 2.4 copy.44
  44.6 0.8 pad_maximum_fusion
  45.4 0.7 copy.33
  46.1 0.6 pad_maximum_fusion.1
  46.7 0.7 copy.36
  47.4 1.7 fusion.33
  49.1 1.5 copy.38
  50.6 0.9 mul.83
  51.5 0.9 mul.86
  52.3 1.5 copy.40
  53.8 0.9 mul.90
  54.7 1.5 copy.41
  56.2 8.1 %convert_reduce_fusion = (f32[1024]{0:T(1024)}, bf16[1536,1024]{1,0:T(8,128)(2,1)S(1)}, f32[1536,1024]{1,0:T(8,128)}) fusion(f32[16,1024]{1,0:T(8,128)} %copy-done.1, f32[1536]{0:T(1024)S(1)} %mul.90, f32[1024]{0:T(1024)} %fusion.24, f32[1536]{0:T(1024)S(1)} %mul.86, f32[1536]{0:T(1024)S(1)} %mul.83, f32[1536,1024]{1,0:T(8,128)} %get-tuple-element.16, ...), kind=kLoop, calls=%fused_computation.9 | loop fusion | flops 14154752 | bytes 15826944 | tf_op jit(solution)/shard_map/reduce_sum | solution.py:82
  64.3 2.7 subtract_multiply_fusion
  67.1 0.9 fusion.31
  68.0 0.9 copy.37
  68.9 0.0 reduce-scatter.5.cloned.1.call-update
  68.9 0.2 all-reduce.4.cloned.1.call-start
  69.2 9.4 %fusion.13 = f32[640,1024]{1,0:T(8,128)} fusion(f32[96,16,1024]{2,1,0:T(8,128)} %bitcast.39, f32[96,16]{0,1:T(8,128)S(1)} %copy-done.9, f32[1024]{0:T(1024)S(1)} %copy-done.5, f32[96,16]{0,1:T(8,128)S(1)} %copy-done.8, f32[96,16]{0,1:T(8,128)S(1)} %copy-done.7, f32[16,1024]{1,0:T(8,128)S(1)} %copy-done.2, f32[16,640]{1,0:T(8,128)S(1)} %copy-done.4, ...), kind=kOutput, calls=%fused_computation.21 | convolution fusion | flops 2024669184 | bytes 9287680 | tf_op jit(solution)/shard_map/dot_general | solution.py:79
  78.5 0.0 all-reduce.4.cloned.1.call-update
  78.6 1.3 dynamic-slice.2
  80.5 106.2 %psum.15 = f32[1024]{0:T(1024)} all-reduce(f32[1024]{0:T(1024)S(1)} %copy-done.6), channel_id=1, replica_groups=mesh['frames'=32,'labels'=16] {'frames','labels'}, use_global_device_ids=true, to_apply=%region_8.9 | all-reduce | flops 1024 | bytes 8192 | tf_op jit(solution)/shard_map/psum | solution.py:85
  186.7 128.3 %all-reduce.1 = f32[16,640]{1,0:T(8,128)S(1)} all-reduce(f32[16,640]{1,0:T(8,128)S(1)} %get-tuple-element.6), channel_id=3, replica_groups=mesh['frames'=32,'labels'=16] {'frames'}, use_global_device_ids=true, to_apply=%region_5.6.clone | all-reduce | flops 10240 | bytes 81920
  315.0 0.7 constant_dynamic-slice_fusion
  315.6 46.8 %all-reduce.4.cloned.1.call-done = f32[640,1024]{1,0:T(8,128)} async-done(((f32[640,1024]{1,0:T(8,128)}), f32[640,1024]{1,0:T(8,128)}) %all-reduce.4.cloned.1.call-update) | async-done | bytes 2621456 | tf_op jit(solution)/shard_map/psum | solution.py:85
  362.4 3.6 copy.58
  (26 shorter events, 0.1 us)
Async XLA Ops:
  8.0 25.4 %copy-start = (bf16[640,1024]{1,0:T(8,128)(2,1)S(1)}, bf16[640,1024]{1,0:T(8,128)(2,1)}, u32[]{:S(2)}) copy-start(bf16[640,1024]{1,0:T(8,128)(2,1)} %param.11) | copy-start | bytes 3932164
  8.0 25.4 %copy-start.10 = (f32[1024]{0:T(1024)S(1)}, f32[1024]{0:T(1024)}, u32[]{:S(2)}) copy-start(f32[1024]{0:T(1024)} %param.12) | copy-start | bytes 12292
  8.0 307.6 %reduce-scatter.5.cloned.1.call-start = ((), (), s32[]{:S(2)}) async-start(), calls=%async_computation.2 | async-start | bytes 348160
  9.4 36.7 %collective-permute-start.1 = (f32[96,1]{0,1:T(1,128)}, f32[96,1]{0,1:T(1,128)}, u32[]{:S(2)}, u32[]{:S(2)}) collective-permute-start(f32[96,1]{0,1:T(1,128)} %slice.27), channel_id=1, source_target_pairs={{1,0},{2,1},{3,2},{4,3},{5,4},{6,5},{7,6},{8,7},{9,8},{10,9},{11,1... | collective-permute-start | bytes 1160 | tf_op jit(solution)/shard_map/ppermute | solution.py:10
  10.7 34.0 %collective-permute-start = (f32[1,16]{0,1:T(8,128)}, f32[1,16]{0,1:T(8,128)}, u32[]{:S(2)}, u32[]{:S(2)}) collective-permute-start(f32[1,16]{0,1:T(8,128)} %bitcast.41), channel_id=1, source_target_pairs={{16,0},{32,16},{48,32},{64,48},{80,64},{96,80},{112,96},{128,112},... | collective-permute-start | bytes 200 | tf_op jit(solution)/shard_map/ppermute | solution.py:10
  29.0 3.1 copy-start.3
  31.2 7.6 %copy-start.1 = (f32[16,1024]{1,0:T(8,128)}, f32[16,1024]{1,0:T(8,128)S(1)}, u32[]{:S(2)}) copy-start(f32[16,1024]{1,0:T(8,128)S(1)} %fusion.16) | copy-start | bytes 196612
  67.0 2.1 copy-start.2
  67.0 2.1 copy-start.4
  67.0 2.1 copy-start.5
  67.0 2.1 copy-start.7
  67.1 2.1 copy-start.8
  67.1 2.1 copy-start.9
  68.9 293.5 %all-reduce.4.cloned.1.call-start = ((), (), s32[]{:S(2)}) async-start(), calls=%async_computation.1 | async-start | bytes 5242880 | tf_op jit(solution)/shard_map/psum | solution.py:85
  69.2 11.3 %copy-start.6 = (f32[1024]{0:T(1024)S(1)}, f32[1024]{0:T(1024)}, u32[]{:S(2)}) copy-start(f32[1024]{0:T(1024)} %get-tuple-element.8) | copy-start | bytes 12292
Sparse Core Ops, SparseCore 0:
  69.0 170.4 reduce-scatter.4
Sparse Core Ops, SparseCore 1:
  78.6 283.7 all-reduce.3
where the time goes:
time: 376 us; the launch traced here: 373 us
  blocking collectives  234 us (62%)
  waiting for transfers between devices  46.8 us (12%)
  local copies, waits for them, and re-layouts  26.9 us (7%)
  other arithmetic  19.8 us (5%)
  between operations  17.6 us (5%)
  matrix products  17.5 us (5%)
  starting transfers between devices  10.3 us (3%)
    unnamed x1, blocking collectives  128 us
    psum x1, blocking collectives, local(): lax.psum((weight_term, bias_term), ('frames', 'labels'))  106 us
    psum x1, waiting for transfers between devices, local(): lax.psum((weight_term, bias_term), ('frames', 'labels'))  46.8 us
    ppermute x2, starting transfers between devices, from_behind(): return lax.ppermute(array, axis, pairs)  10.1 us
    dot_general x1, matrix products, local(): lax.dot_general(joint, grad_logits, (((0,), (0,)), ((), ())), preferred_e...  9.35 us
    unnamed x27, local copies, waits for them, and re-layouts  9.34 us
    reduce_sum x1, other arithmetic, local(): bias_term = jnp.sum(grad_logits.astype(jnp.float32), axis=0)  8.1 us
  transfers between devices with their start and end apart: 4, of which 1 were waited for; matrix products, arithmetic and copies ran while one was open for 10% of the time, Pallas kernels for 0%

commit v1 on v0

v1 whole, which is shorter than its diff:
```python
import functools

import jax
import jax.numpy as jnp
from jax import lax
from jax.experimental import pallas as pl
from jax.experimental.pallas import tpu as pltpu
from jax.sharding import PartitionSpec as P

MESH = pl.DeviceIdType.MESH
FR, LB, H, V = 96, 16, 640, 1024
GU = 4
ROWS = FR * GU
NX, NY, NZ = 4, 8, 8
HALF = 2560
A1, B, A2, C = 0, 768, 1280, 2048
F32, BF16 = jnp.float32, jnp.bfloat16


def place(x, y, z, c):
    return (x * 8 + (y % 4) * 2 + c, z * 2 + y // 4)


def rows(ref, start, size):
    return ref.at[pl.ds(pl.multiple_of(start, 8), size)]


def kernel(
    enc_ref, pred_ref, w_ref, bias_ref, labels_ref, lengths_ref, alpha_ref, beta_ref, ll_ref,
    out_ref, bias_out, enc_out, pred_out,
    encf, predf, joint, expo, grad, bsend, brow, bcol, asave, ssum, slab, sblank, occb, occl,
    bias_acc, peer_half, core_recv, acc, send_b,
    r1a1, r1b, r1a2, r1c, s1a1, s1a2, s1c, s2b, r2a1, r2b, r2a2, r2c,
    r3a1, r3b, r3a2, r3c,
    enc_acc, enc_t, e1_recv, e1_sum, e2_recv, tsq, pred_acc, pbuf, p1_recv, p2_recv, p3_recv,
    ssem, rsem,
):
    f = lax.axis_index("frames")
    l = lax.axis_index("labels")
    x, ylo, c = f // 8, (f // 2) % 4, f % 2
    z, yhi = l // 2, l % 2
    y = yhi * 4 + ylo
    other = 1 - c
    sibling = place(x, y, z, other)

    def xp(r):
        return place((x + r) % NX, y, z, c)

    def yp(r):
        return place(x, (y + r) % NY, z, c)

    def zp(r):
        return place(x, y, (z + r) % NZ, c)

    def send(src, dst, s, to):
        pltpu.make_async_remote_copy(
            src_ref=src, dst_ref=dst, send_sem=ssem.at[s], recv_sem=rsem.at[s],
            device_id=to, device_id_type=MESH,
        ).start()

    def arrived(s, ref):
        pltpu.make_async_copy(ref, ref, rsem.at[s]).wait()

    def left(s, ref):
        pltpu.make_async_copy(ref, ref, ssem.at[s]).wait()

    barrier = pltpu.get_barrier_semaphore()
    peers = [sibling]
    peers += [xp(r) for r in range(1, NX)] + [yp(r) for r in range(1, NY)] + [zp(r) for r in range(1, NZ)]
    peers += [((f + 1) % 32, l), (f, (l + 1) % 16)]
    for p in peers:
        pl.semaphore_signal(barrier, inc=1, device_id=p, device_id_type=MESH)

    encf[...] = enc_ref[...].astype(F32)
    predf[...] = pred_ref[...].astype(F32)
    bsend[...] = jnp.zeros_like(bsend)
    bsend[:, 0:LB] = beta_ref[...]
    asave[...] = jnp.zeros_like(asave)
    asave[:, 0:LB] = alpha_ref[...]
    ssum[...] = jnp.ones_like(ssum)
    slab[...] = jnp.zeros_like(slab)
    sblank[...] = jnp.zeros_like(sblank)
    lane = lax.broadcasted_iota(jnp.int32, (1, 128), 1)
    vocab = lax.broadcasted_iota(jnp.int32, (1, V), 1)

    def forward(g, _):
        for k in range(GU):
            u = g * GU + k
            start = pl.multiple_of(u * FR, 32)
            joint[pl.ds(start, FR)] = jnp.tanh(encf[...] + predf[pl.ds(u, 1)]).astype(BF16)
        first = pl.multiple_of(g * ROWS, 128)
        logits = jnp.dot(joint[pl.ds(first, ROWS)], w_ref[...], preferred_element_type=F32) + bias_ref[...]
        for k in range(GU):
            u = g * GU + k
            start = pl.multiple_of(u * FR, 32)
            part = logits[k * FR:(k + 1) * FR]
            e = jnp.exp(part)
            expo[pl.ds(start, FR)] = e
            hot = vocab == labels_ref[u]
            here = lane == u
            ssum[...] = jnp.where(here, jnp.sum(e, axis=1, keepdims=True), ssum[...])
            slab[...] = jnp.where(here, jnp.sum(jnp.where(hot, part, 0.0), axis=1, keepdims=True), slab[...])
            sblank[...] = jnp.where(here, part[:, 0:1], sblank[...])
        return 0

    forward(0, 0)
    pl.semaphore_wait(barrier, len(peers))
    send(bsend.at[pl.ds(0, 8)], brow, 0, ((f + 31) % 32, l))
    send(bsend, bcol, 1, (f, (l + 15) % 16))
    lax.fori_loop(1, LB // GU, forward, 0)

    arrived(0, brow)
    arrived(1, bcol)
    frame_len, label_len, log_total = lengths_ref[0], lengths_ref[1], ll_ref[0]
    t_here = lax.broadcasted_iota(jnp.int32, (FR, 128), 0)
    u_here = lax.broadcasted_iota(jnp.int32, (FR, 128), 1)
    t_pos, u_pos = t_here + f * FR, u_here + l * LB
    beta = bsend[...]
    beta_frame = jnp.where(t_here == FR - 1, brow[0:1, :], pltpu.roll(beta, FR - 1, 0))
    beta_label = jnp.where(u_here == LB - 1, bcol[:, 0:1], pltpu.roll(beta, 127, 1))
    total = ssum[...]
    lse = jnp.log(total)
    inner = (t_pos < frame_len - 1) & (u_pos <= label_len)
    final = (t_pos == frame_len - 1) & (u_pos == label_len)
    blank_ok = (inner | final) & (u_here < LB)
    blank_arg = asave[...] + (sblank[...] - lse) + jnp.where(inner, beta_frame, 0.0) - log_total
    occb[...] = jnp.where(blank_ok, jnp.exp(jnp.where(blank_ok, blank_arg, 0.0)), 0.0)
    label_ok = (t_pos < frame_len) & (u_pos < label_len) & (u_here < LB)
    label_arg = asave[...] + (slab[...] - lse) + beta_label - log_total
    occl[...] = jnp.where(label_ok, jnp.exp(jnp.where(label_ok, label_arg, 0.0)), 0.0)
    ssum[...] = 4.0 / total

    bias_acc[...] = jnp.zeros_like(bias_acc)

    def backward(u, _):
        here = lane == u
        start = pl.multiple_of(u * FR, 32)

        def column(ref):
            return jnp.sum(jnp.where(here, ref[...], 0.0), axis=1, keepdims=True)

        blank, label, inverse = column(occb), column(occl), column(ssum)
        quarter = (blank + label) * 0.25
        hot = vocab == labels_ref[u]
        g = (expo[pl.ds(start, FR)] * inverse) * quarter
        g = jnp.where(hot, g - label, g)
        g0 = jnp.where(lane == 0, g[:, 0:128] - blank, g[:, 0:128])
        grad[pl.ds(start, FR)] = g.astype(BF16)
        grad[pl.ds(start, FR), 0:128] = g0.astype(BF16)
        bias_acc[:, 128:] += jnp.sum(g[:, 128:].reshape(FR // 8, 8, V - 128), axis=0)
        bias_acc[:, 0:128] += jnp.sum(g0.reshape(FR // 8, 8, 128), axis=0)
        return 0

    lax.fori_loop(0, LB, backward, 0)

    def product(half, q, ref):
        base = pl.multiple_of(half * 512 + q * 256, 256)
        r = lax.dot_general(
            joint[...], grad[:, pl.ds(base, 256)], (((0,), (0,)), ((), ())), preferred_element_type=F32
        )
        ref[q * 1280:q * 1280 + 640] = r[:, 0:128]
        ref[q * 1280 + 640:q * 1280 + 1280] = r[:, 128:256]

    for q in range(2):
        product(other, q, peer_half)
        if q == 0:
            for k in range(8):
                peer_half[HALF + k:HALF + k + 1] = jnp.sum(bias_acc[:, k * 128:(k + 1) * 128], axis=0, keepdims=True)
            acc[HALF:HALF + 8] = peer_half[HALF:HALF + 8]
            send(rows(peer_half, HALF, 8), rows(core_recv, HALF, 8), 2, sibling)
        send(rows(peer_half, q * 1280, 1280), rows(core_recv, q * 1280, 1280), 3 + q, sibling)
    product(c, 0, acc)

    arrived(2, rows(core_recv, HALF, 8))
    arrived(3, rows(core_recv, 0, 1280))
    acc[0:768] += core_recv[0:768]
    for r in (2, 1, 3):
        send(rows(acc, A1 + (x + r) % NX * 192, 192), r1a1.at[r - 1], 5, xp(r))
    bias_tile = acc[HALF:HALF + 8] + core_recv[HALF:HALF + 8]
    for k in range(NY):
        send_b[k, 0:64] = acc[B + k * 64:B + k * 64 + 64] + core_recv[B + k * 64:B + k * 64 + 64]
        send_b[k, 64:72] = bias_tile
    for r in (4, 3, 5, 2, 6, 1, 7):
        send(send_b.at[(y + r) % NY], r1b.at[y], 6, yp(r))
    product(c, 1, acc)
    arrived(4, rows(core_recv, 1280, 1280))
    acc[1280:2560] += core_recv[1280:2560]
    for r in (2, 1, 3):
        send(rows(acc, A2 + (x + r) % NX * 192, 192), r1a2.at[r - 1], 7, xp(r))
    for r in (4, 3, 5, 2, 6, 1, 7):
        send(rows(acc, C + (z + r) % NZ * 64, 64), r1c.at[r - 1], 8, zp(r))
    r1b[y] = send_b[y]

    enc_acc[...] = jnp.zeros_like(enc_acc)

    def pre(g, _):
        first = pl.multiple_of(g * ROWS, 128)
        gj = lax.dot_general(
            grad[pl.ds(first, ROWS)], w_ref[...], (((1,), (1,)), ((), ())), preferred_element_type=F32
        )
        j = joint[pl.ds(first, ROWS)].astype(F32)
        gp = gj * (1.0 - j * j)
        enc_acc[0:FR] += (gp[0:FR] + gp[FR:2 * FR]) + (gp[2 * FR:3 * FR] + gp[3 * FR:4 * FR])
        for k in range(GU):
            pred_acc[pl.ds(g * GU + k, 1), 0:H] = jnp.sum(gp[k * FR:(k + 1) * FR], axis=0, keepdims=True)
        return 0

    pred_acc[...] = jnp.zeros_like(pred_acc)
    lax.fori_loop(0, LB // GU, pre, 0)
    for k in range(5):
        enc_t[k * 128:(k + 1) * 128] = jnp.transpose(enc_acc[:, k * 128:(k + 1) * 128])
    wide = pred_acc[...]
    for cc in range(2):
        for xx in range(4):
            for yy in range(4):
                start = (xx * 8 + yy * 2 + cc) * 20
                lo = start // 128 * 128
                two = wide[:, lo:lo + 256]
                pbuf[cc, xx, yy] = pltpu.roll(two, (256 - (start - lo)) % 256, 1)[:, 0:128]
    send(pbuf.at[other], p1_recv, 9, sibling)

    arrived(5, r1a1)
    s1a1[...] = (rows(acc, A1 + x * 192, 192)[...] + r1a1[0]) + (r1a1[1] + r1a1[2])
    for r in (4, 3, 5, 2, 6, 1, 7):
        send(rows(s1a1, (y + r) % NY * 24, 24), r2a1.at[r - 1], 10, yp(r))
    arrived(6, r1b.at[pl.ds(0, 7)])
    sum_b = r1b[0]
    for k in range(1, NY):
        sum_b = sum_b + r1b[k]
    for k in range(NZ):
        s2b[k, 0:8] = sum_b[k * 8:k * 8 + 8]
        s2b[k, 8:16] = sum_b[64:72]
    for r in (4, 3, 5, 2, 6, 1, 7):
        send(s2b.at[(z + r) % NZ], r2b.at[z], 11, zp(r))
    arrived(7, r1a2)
    s1a2[...] = (rows(acc, A2 + x * 192, 192)[...] + r1a2[0]) + (r1a2[1] + r1a2[2])
    for r in (4, 3, 5, 2, 6, 1, 7):
        send(rows(s1a2, (z + r) % NZ * 24, 24), r2a2.at[r - 1], 12, zp(r))
    arrived(8, r1c)
    sum_c = rows(acc, C + z * 64, 64)[...]
    for k in range(7):
        sum_c = sum_c + r1c[k]
    s1c[...] = sum_c
    for r in (4, 3, 5, 2, 6, 1, 7):
        send(rows(s1c, (y + r) % NY * 8, 8), r2c.at[r - 1], 13, yp(r))
    r2b[z] = s2b[z]

    for r in (4, 3, 5, 2, 6, 1, 7):
        send(rows(enc_t, (z + r) % NZ * 80, 80), e1_recv.at[r - 1], 14, zp(r))
    arrived(9, p1_recv)
    pbuf[c] = pbuf[c] + p1_recv[...]
    for r in (2, 1, 3):
        send(pbuf.at[c, (x + r) % NX], p2_recv.at[r - 1], 15, xp(r))

    arrived(10, r2a1)
    sum_a = rows(s1a1, y * 24, 24)[...]
    for k in range(7):
        sum_a = sum_a + r2a1[k]
    r3a1[z] = sum_a
    for r in (4, 3, 5, 2, 6, 1, 7):
        send(r3a1.at[z], r3a1.at[z], 16, zp(r))
    arrived(12, r2a2)
    sum_a = rows(s1a2, z * 24, 24)[...]
    for k in range(7):
        sum_a = sum_a + r2a2[k]
    r3a2[y] = sum_a
    for r in (4, 3, 5, 2, 6, 1, 7):
        send(r3a2.at[y], r3a2.at[y], 17, yp(r))
    arrived(11, r2b.at[pl.ds(0, 7)])
    sum_b = r2b[0]
    for k in range(1, NZ):
        sum_b = sum_b + r2b[k]
    r3b[x] = sum_b
    for r in (2, 1, 3):
        send(r3b.at[x], r3b.at[x], 18, xp(r))
    arrived(13, r2c)
    sum_c = rows(s1c, y * 8, 8)[...]
    for k in range(7):
        sum_c = sum_c + r2c[k]
    r3c[x] = sum_c
    for r in (2, 1, 3):
        send(r3c.at[x], r3c.at[x], 19, xp(r))

    base = c * HALF

    def spread(start, size, s, peer, order):
        piece = rows(out_ref, base + start, size)
        for r in order:
            send(piece, piece, s, peer(r))

    far8, far4 = (4, 3, 5, 2, 6, 1, 7), (2, 1, 3)
    arrived(16, r3a1.at[pl.ds(0, 7)])
    sum_a = r3a1[0]
    for k in range(1, NZ):
        sum_a = sum_a + r3a1[k]
    rows(out_ref, base + A1 + (x * 8 + y) * 24, 24)[...] = sum_a
    spread(A1 + (x * 8 + y) * 24, 24, 20, yp, far8)
    arrived(17, r3a2.at[pl.ds(0, 7)])
    sum_a = r3a2[0]
    for k in range(1, NY):
        sum_a = sum_a + r3a2[k]
    rows(out_ref, base + A2 + (x * 8 + z) * 24, 24)[...] = sum_a
    spread(A2 + (x * 8 + z) * 24, 24, 21, zp, far8)
    arrived(18, r3b.at[pl.ds(0, 3)])
    sum_b = (r3b[0] + r3b[1]) + (r3b[2] + r3b[3])
    rows(out_ref, base + B + (y * 8 + z) * 8, 8)[...] = sum_b[0:8]
    bias_out[...] = sum_b[8:16]
    spread(B + (y * 8 + z) * 8, 8, 22, zp, far8)
    arrived(19, r3c.at[pl.ds(0, 3)])
    rows(out_ref, base + C + (z * 8 + y) * 8, 8)[...] = (r3c[0] + r3c[1]) + (r3c[2] + r3c[3])
    spread(C + (z * 8 + y) * 8, 8, 23, yp, far8)

    arrived(14, e1_recv)
    e = rows(enc_t, z * 80, 80)[...]
    for k in range(7):
        e = e + e1_recv[k]
    e1_sum[...] = e
    send(rows(e1_sum, (1 - yhi) * 40, 40), e2_recv, 24, yp(4))
    arrived(15, p2_recv)
    pbuf[c, x] = (pbuf[c, x] + p2_recv[0]) + (p2_recv[1] + p2_recv[2])
    for r in (2, 1, 3):
        to = (ylo + r) % 4
        send(pbuf.at[c, x, to], p3_recv.at[r - 1], 25, place(x, yhi * 4 + to, z, c))

    arrived(20, rows(out_ref, 0, 168))
    spread(A1 + x * 192, 192, 26, xp, far4)
    arrived(21, rows(out_ref, 0, 168))
    spread(A2 + x * 192, 192, 27, xp, far4)
    arrived(22, rows(out_ref, 0, 56))
    spread(B + y * 64, 64, 28, yp, far8)
    arrived(23, rows(out_ref, 0, 56))
    spread(C + z * 64, 64, 29, zp, far8)

    arrived(24, e2_recv)
    tsq[...] = jnp.zeros_like(tsq)
    tsq[0:40] = rows(e1_sum, yhi * 40, 40)[...] + e2_recv[...]
    enc_out[...] = jnp.transpose(tsq[...])[0:FR, 0:40]
    arrived(25, p3_recv)
    pred_out[...] = ((pbuf[c, x, ylo] + p3_recv[0]) + (p3_recv[1] + p3_recv[2]))[:, 0:20]

    arrived(26, rows(out_ref, 0, 576))
    send(rows(out_ref, base + A1, 768), rows(out_ref, base + A1, 768), 30, sibling)
    arrived(27, rows(out_ref, 0, 576))
    send(rows(out_ref, base + A2, 768), rows(out_ref, base + A2, 768), 31, sibling)
    arrived(28, rows(out_ref, 0, 448))
    send(rows(out_ref, base + B, 512), rows(out_ref, base + B, 512), 32, sibling)
    arrived(29, rows(out_ref, 0, 448))
    send(rows(out_ref, base + C, 512), rows(out_ref, base + C, 512), 33, sibling)
    for s, n in ((30, 768), (31, 768), (32, 512), (33, 512)):
        arrived(s, rows(out_ref, 0, n))

    left(0, brow)
    left(1, bcol)
    for s, n in (
        (2, 8), (3, 1280), (4, 1280), (5, 576), (6, 504), (7, 576), (8, 448), (10, 168), (11, 112), (12, 168),
        (13, 56), (14, 560), (16, 168), (17, 168), (18, 48), (19, 24), (20, 168), (21, 168), (22, 56), (23, 56),
        (24, 40), (26, 576), (27, 576), (28, 448), (29, 448), (30, 768), (31, 768), (32, 512), (33, 512),
    ):
        left(s, rows(out_ref, 0, n))
    left(9, p1_recv)
    left(15, p2_recv)
    left(25, p3_recv)


def vm(*shape, dtype=F32):
    return pltpu.VMEM(shape, dtype)


def local(encoder_out, predictor_out, out_weight, out_bias, target_labels, lengths, alpha, beta, log_likelihood):
    vmem = pl.BlockSpec(memory_space=pltpu.VMEM)
    smem = pl.BlockSpec(memory_space=pltpu.SMEM)
    weight, bias, enc, pred = pl.pallas_call(
        kernel,
        out_shape=(
            jax.ShapeDtypeStruct((2 * HALF, 128), F32),
            jax.ShapeDtypeStruct((8, 128), F32),
            jax.ShapeDtypeStruct((FR, 40), F32),
            jax.ShapeDtypeStruct((LB, 20), F32),
        ),
        in_specs=[vmem, vmem, vmem, vmem, smem, smem, vmem, vmem, smem],
        out_specs=(vmem, vmem, vmem, vmem),
        scratch_shapes=[
            vm(FR, H), vm(LB, H), vm(FR * LB, H, dtype=BF16), vm(FR * LB, V), vm(FR * LB, V, dtype=BF16),
            vm(FR, 128), vm(8, 128), vm(FR, 128), vm(FR, 128), vm(FR, 128), vm(FR, 128), vm(FR, 128),
            vm(FR, 128), vm(FR, 128),
            vm(8, V), vm(HALF + 8, 128), vm(HALF + 8, 128), vm(HALF + 8, 128), vm(8, 72, 128),
            vm(3, 192, 128), vm(8, 72, 128), vm(3, 192, 128), vm(7, 64, 128),
            vm(192, 128), vm(192, 128), vm(64, 128), vm(8, 16, 128),
            vm(7, 24, 128), vm(8, 16, 128), vm(7, 24, 128), vm(7, 8, 128),
            vm(8, 24, 128), vm(4, 16, 128), vm(8, 24, 128), vm(4, 8, 128),
            vm(128, H), vm(H, 128), vm(7, 80, 128), vm(80, 128), vm(40, 128), vm(128, 128),
            vm(LB, 768), vm(2, 4, 4, LB, 128), vm(4, 4, LB, 128), vm(3, 4, LB, 128), vm(3, LB, 128),
            pltpu.SemaphoreType.DMA((34,)), pltpu.SemaphoreType.DMA((34,)),
        ],
        compiler_params=pltpu.CompilerParams(
            collective_id=0, has_side_effects=True, vmem_limit_bytes=56 * 2**20
        ),
        name="joint_backward",
    )(
        encoder_out, predictor_out, out_weight, out_bias.reshape(1, V), target_labels, lengths, alpha, beta,
        log_likelihood,
    )
    grad_weight = weight.reshape(8, H, 128).transpose(1, 0, 2).reshape(H, V)
    return enc, pred, grad_weight, bias.reshape(V)


def solution(mesh):
    placed = (
        P("frames", None), P("labels", None), P(), P(), P("labels"), P(),
        P("frames", "labels"), P("frames", "labels"), P(),
    )
    return jax.shard_map(
        local,
        mesh=mesh,
        in_specs=placed,
        out_specs=(P("frames", "labels"), P("labels", "frames"), P(), P()),
        check_vma=False,
    )
```

time: 376 us -> 83.8 us (0.22)
  blocking collectives: 234 us -> 0 us
  Pallas kernels: 0 us -> 73.1 us
  waiting for transfers between devices: 46.8 us -> 0 us
  other arithmetic: 19.8 us -> 0 us
  local copies, waits for them, and re-layouts: 26.9 us -> 9.09 us
  matrix products: 17.5 us -> 0 us
  between operations: 17.6 us -> 1.29 us
  starting transfers between devices: 10.3 us -> 0 us
    unnamed x1 -> x0, blocking collectives: 128 us -> none
    psum x1 -> x0, blocking collectives: 106 us -> none  [local(): lax.psum((weight_term, bias_term), ('frames', 'labels'))]
    pallas_call x0 -> x1, Pallas kernels: none -> 73.1 us  [local(): pl.pallas_call(kernel, out_shape=(jax.ShapeDtypeStruct((2 * HALF, 128), F...]
    psum x1 -> x0, waiting for transfers between devices: 46.8 us -> none  [local(): lax.psum((weight_term, bias_term), ('frames', 'labels'))]
    dot_general x3 -> x0, matrix products: 17.5 us -> none  [the longest x1 9.35 us: local(): lax.dot_general(joint, grad_logits, (((0,), (0,)), ((), ())), preferred_e...]
    ppermute x2 -> x0, starting transfers between devices: 10.1 us -> none  [from_behind(): return lax.ppermute(array, axis, pairs)]
    reduce_sum x2 -> x0, other arithmetic: 8.99 us -> none  [the longest x1 8.1 us: local(): bias_term = jnp.sum(grad_logits.astype(jnp.float32), axis=0)]
    slice x5 -> x0, local copies, waits for them, and re-layouts: 6.16 us -> none  [the longest x1 2.06 us: local(): lp_blank = logits3[:, :, 0] - lse2]
  transfers between devices with their start and end apart: 4 -> 0, of which waited for: 1 -> 0; matrix products, arithmetic and copies ran while one was open for 10% -> 0% of each run, Pallas kernels for 0% -> 0%
where the time goes in v1:
time: 83.8 us; the launch traced here: 83.5 us
  Pallas kernels  73.1 us (87%)
  local copies, waits for them, and re-layouts  9.09 us (11%)
  between operations  1.29 us (2%)
    pallas_call x1, Pallas kernels, local(): pl.pallas_call(kernel, out_shape=(jax.ShapeDtypeStruct((2 * HALF, 128), F...  73.1 us
    unnamed x9, local copies, waits for them, and re-layouts  5.49 us
    reshape x1, local copies, waits for them, and re-layouts, local(): grad_weight = weight.reshape(8, H, 128).transpose(1, 0, 2).reshape(H, V)  3.6 us

profile of v1, /device:TPU:1, one launch (start us, length us, event | category | flops | bytes accessed | tf_op | source)
XLA Modules:
  0.0 83.5 jit_solution(9157444740504826004)
XLA Ops:
  1.3 1.4 %copy.13.alpha_ref = f32[96,16]{1,0:T(8,128)} copy(f32[96,16]{0,1:T(8,128)} %param.15) | data formatting | bytes 12288 | tf_op args[6]
  2.7 1.4 %copy.14.beta_ref = f32[96,16]{1,0:T(8,128)} copy(f32[96,16]{0,1:T(8,128)} %param.16) | data formatting | bytes 12288 | tf_op args[7]
  4.1 73.1 %joint_backward.1 = (f32[5120,128]{1,0:T(8,128)}, f32[8,128]{1,0:T(8,128)}, f32[96,40]{1,0:T(8,128)}, f32[16,20]{1,0:T(8,128)}) custom-call(bf16[96,640]{1,0:T(8,128)(2,1)} %enc_ref.1, bf16[16,640]{1,0:T(8,128)(2,1)} %pred_ref.1, bf16[640,1024]{1,0:T(8,128)(2,1)} %w_ref.1, f32[1,1024]{1,0:T(1,128)} %bitcast.11, s32[16]{0:T(128)} %labels_ref.1, ...), custom_call_target="tpu_custom_call" | custom-call | tf_op jit(solution)/shard_map/joint_backward/pallas_call | solution.py:372
  77.2 1.5 %copy.16 = f32[96,40]{0,1:T(8,128)} copy(f32[96,40]{1,0:T(8,128)} %get-tuple-element.12) | data formatting | bytes 30720
  78.7 0.0 copy-start
  78.7 0.0 copy-start.1
  78.7 3.6 %copy.19 = f32[8,80,8,128]{3,2,0,1:T(8,128)} copy(f32[8,80,8,128]{3,2,1,0:T(8,128)} %bitcast.10) | data formatting | bytes 5242880 | tf_op jit(solution)/shard_map/reshape | solution.py:403
  82.3 0.0 copy-done
  82.3 0.6 copy.23
  82.9 0.0 copy-done.1
  82.9 0.6 copy.24
Async XLA Ops:
  78.7 3.6 %copy-start = (f32[16,20]{1,0:T(8,128)S(1)}, f32[16,20]{1,0:T(8,128)}, u32[]{:S(2)}) copy-start(f32[16,20]{1,0:T(8,128)} %get-tuple-element.21) | copy-start | bytes 3844
  78.7 4.2 %copy-start.1 = (f32[8,128]{1,0:T(8,128)S(1)}, f32[8,128]{1,0:T(8,128)}, u32[]{:S(2)}) copy-start(f32[8,128]{1,0:T(8,128)} %get-tuple-element.11) | copy-start | bytes 12292

commit v2 on v1

v2 whole, which is shorter than its diff:
```python
import jax
import jax.numpy as jnp
from jax import lax
from jax.experimental import pallas as pl
from jax.experimental.pallas import tpu as pltpu
from jax.sharding import PartitionSpec as P

MESH = pl.DeviceIdType.MESH
FR, LB, H, V = 96, 16, 640, 1024
GU = 4
ROWS = FR * GU
NX, NY, NZ = 4, 8, 8
HALF = 2560
A1, B, A2, C = 0, 768, 1280, 2048
SEMS = 80
F32, BF16 = jnp.float32, jnp.bfloat16


def place(x, y, z, c):
    return (x * 8 + (y % 4) * 2 + c, z * 2 + y // 4)


def rows(ref, start, size):
    return ref.at[pl.ds(pl.multiple_of(start, 8), size)]


def kernel(
    enc_in, pred_in, w_in, bias_in, labels_in, lengths_in, alpha_in, beta_in, ll_ref,
    out_ref, bias_out, enc_out, pred_out,
    enc_ref, pred_ref, w_ref, bias_ref, labels_ref, lengths_ref, alpha_ref, beta_ref, isem,
    encf, predf, joint, expo, grad, bsend, brow, bcol, turn, ssum, slab, sblank, occb, occl,
    bias_acc, peer_half, core_recv, acc, send_b,
    r1a1, r1b, r1a2, r1c, s1a1, s1a2, s1c, s2b, r2a1, r2b, r2a2, r2c,
    r3a1, r3b, r3a2, r3c,
    enc_acc, enc_t, e_up, e_down, e_sum, e_last, pred_acc, pbuf, p1_recv, p2_recv, p3_recv,
    ssem, rsem,
):
    f = lax.axis_index("frames")
    l = lax.axis_index("labels")
    x, ylo, c = f // 8, (f // 2) % 4, f % 2
    z, yhi = l // 2, l % 2
    y = yhi * 4 + ylo
    other = 1 - c
    sibling = place(x, y, z, other)
    far8, near8, far4, near4 = (4, 3, 5, 2, 6, 1, 7), (1, 7, 2, 6, 3, 5, 4), (2, 1, 3), (1, 3, 2)

    def xp(r):
        return place((x + r) % NX, y, z, c)

    def yp(r):
        return place(x, (y + r) % NY, z, c)

    def zp(r):
        return place(x, y, (z + r) % NZ, c)

    index, amount = {}, {}

    def send(src, dst, kind, to):
        k = index.setdefault(kind, len(index))
        size = 1
        for n in src.shape[:-1]:
            size *= n
        amount[kind] = amount.get(kind, 0) + size
        pltpu.make_async_remote_copy(
            src_ref=src, dst_ref=dst, send_sem=ssem.at[k], recv_sem=rsem.at[k],
            device_id=to, device_id_type=MESH,
        ).start()

    def wait(sem, kind):
        ref = out_ref.at[pl.ds(0, amount[kind])]
        pltpu.make_async_copy(ref, ref, sem.at[index[kind]]).wait()

    def arrived(kind):
        wait(rsem, kind)

    loads = [
        pltpu.make_async_copy(src, dst, isem.at[k])
        for k, (src, dst) in enumerate((
            (enc_in, enc_ref), (pred_in, pred_ref), (beta_in, beta_ref), (alpha_in, alpha_ref), (bias_in, bias_ref),
            (labels_in, labels_ref), (lengths_in, lengths_ref), (w_in, w_ref),
        ))
    ]
    for load in loads:
        load.start()

    barrier = pltpu.get_barrier_semaphore()
    peers = [sibling]
    peers += [xp(r) for r in range(1, NX)] + [yp(r) for r in range(1, NY)] + [zp(r) for r in range(1, NZ)]
    peers += [((f + 1) % 32, l), (f, (l + 1) % 16)]
    for p in peers:
        pl.semaphore_signal(barrier, inc=1, device_id=p, device_id_type=MESH)

    for load in loads:
        load.wait()

    encf[...] = enc_ref[...].astype(F32)
    predf[...] = pred_ref[...].astype(F32)
    bsend[...] = jnp.zeros_like(bsend)
    bsend[:, 0:FR] = beta_ref[...]
    turn[...] = jnp.zeros_like(turn)
    turn[0, 0:LB, 0:FR] = alpha_ref[...]
    ssum[...] = jnp.ones_like(ssum)
    slab[...] = jnp.zeros_like(slab)
    sblank[...] = jnp.zeros_like(sblank)
    lane = lax.broadcasted_iota(jnp.int32, (1, 128), 1)
    vocab = lax.broadcasted_iota(jnp.int32, (1, V), 1)

    def forward(g, _):
        for k in range(GU):
            u = g * GU + k
            start = pl.multiple_of(u * FR, 32)
            joint[pl.ds(start, FR)] = jnp.tanh(encf[...] + predf[pl.ds(u, 1)]).astype(BF16)
        first = pl.multiple_of(g * ROWS, 128)
        logits = jnp.dot(joint[pl.ds(first, ROWS)], w_ref[...], preferred_element_type=F32) + bias_ref[...]
        for k in range(GU):
            u = g * GU + k
            start = pl.multiple_of(u * FR, 32)
            part = logits[k * FR:(k + 1) * FR]
            e = jnp.exp(part)
            expo[pl.ds(start, FR)] = e
            hot = vocab == labels_ref[u]
            here = lane == u
            ssum[...] = jnp.where(here, jnp.sum(e, axis=1, keepdims=True), ssum[...])
            slab[...] = jnp.where(here, jnp.sum(jnp.where(hot, part, 0.0), axis=1, keepdims=True), slab[...])
            sblank[...] = jnp.where(here, part[:, 0:1], sblank[...])
        return 0

    forward(0, 0)
    pl.semaphore_wait(barrier, len(peers))
    send(bsend, brow, "frame", ((f + 31) % 32, l))
    send(bsend.at[pl.ds(0, 8)], bcol, "label", (f, (l + 15) % 16))
    lax.fori_loop(1, LB // GU, forward, 0)

    arrived("frame")
    arrived("label")
    frame_len, label_len, log_total = lengths_ref[0], lengths_ref[1], ll_ref[0]
    beta = bsend[...]
    label_row = lax.broadcasted_iota(jnp.int32, (LB, 128), 0)
    turn[1, 0:LB] = jnp.where(lane == FR - 1, brow[:, 0:1], pltpu.roll(beta, 127, 1))
    turn[2, 0:LB] = jnp.where(label_row == LB - 1, bcol[0:1, :], pltpu.roll(beta, LB - 1, 0))
    alpha = jnp.transpose(turn[0])[0:FR]
    beta_frame = jnp.transpose(turn[1])[0:FR]
    beta_label = jnp.transpose(turn[2])[0:FR]
    t_pos = lax.broadcasted_iota(jnp.int32, (FR, 128), 0) + f * FR
    u_here = lax.broadcasted_iota(jnp.int32, (FR, 128), 1)
    u_pos = u_here + l * LB
    total = ssum[...]
    lse = jnp.log(total)
    inner = (t_pos < frame_len - 1) & (u_pos <= label_len)
    final = (t_pos == frame_len - 1) & (u_pos == label_len)
    blank_ok = (inner | final) & (u_here < LB)
    blank_arg = alpha + (sblank[...] - lse) + jnp.where(inner, beta_frame, 0.0) - log_total
    occb[...] = jnp.where(blank_ok, jnp.exp(jnp.where(blank_ok, blank_arg, 0.0)), 0.0)
    label_ok = (t_pos < frame_len) & (u_pos < label_len) & (u_here < LB)
    label_arg = alpha + (slab[...] - lse) + beta_label - log_total
    occl[...] = jnp.where(label_ok, jnp.exp(jnp.where(label_ok, label_arg, 0.0)), 0.0)
    ssum[...] = 4.0 / total

    bias_acc[...] = jnp.zeros_like(bias_acc)

    def backward(u, _):
        here = lane == u
        start = pl.multiple_of(u * FR, 32)

        def column(ref):
            return jnp.sum(jnp.where(here, ref[...], 0.0), axis=1, keepdims=True)

        blank, label, inverse = column(occb), column(occl), column(ssum)
        quarter = (blank + label) * 0.25
        hot = vocab == labels_ref[u]
        g = (expo[pl.ds(start, FR)] * inverse) * quarter
        g = jnp.where(hot, g - label, g)
        g0 = jnp.where(lane == 0, g[:, 0:128] - blank, g[:, 0:128])
        grad[pl.ds(start, FR)] = g.astype(BF16)
        grad[pl.ds(start, FR), 0:128] = g0.astype(BF16)
        bias_acc[:, 128:] += jnp.sum(g[:, 128:].reshape(FR // 8, 8, V - 128), axis=0)
        bias_acc[:, 0:128] += jnp.sum(g0.reshape(FR // 8, 8, 128), axis=0)
        return 0

    lax.fori_loop(0, LB, backward, 0)

    def product(half, q, ref):
        base = pl.multiple_of(half * 512 + q * 256, 256)
        r = lax.dot_general(
            joint[...], grad[:, pl.ds(base, 256)], (((0,), (0,)), ((), ())), preferred_element_type=F32
        )
        ref[q * 1280:q * 1280 + 640] = r[:, 0:128]
        ref[q * 1280 + 640:q * 1280 + 1280] = r[:, 128:256]

    for q in range(2):
        product(other, q, peer_half)
        if q == 0:
            for k in range(8):
                peer_half[HALF + k:HALF + k + 1] = jnp.sum(bias_acc[:, k * 128:(k + 1) * 128], axis=0, keepdims=True)
            acc[HALF:HALF + 8] = peer_half[HALF:HALF + 8]
            send(rows(peer_half, HALF, 8), rows(core_recv, HALF, 8), "bias", sibling)
        send(rows(peer_half, q * 1280, 1280), rows(core_recv, q * 1280, 1280), ("half", q), sibling)
    product(c, 0, acc)

    arrived("bias")
    arrived(("half", 0))
    acc[0:768] += core_recv[0:768]
    for r in far4:
        send(rows(acc, A1 + (x + r) % NX * 192, 192), r1a1.at[r - 1], "a1 1", xp(r))
    bias_tile = acc[HALF:HALF + 8] + core_recv[HALF:HALF + 8]
    for k in range(NY):
        send_b[k, 0:64] = acc[B + k * 64:B + k * 64 + 64] + core_recv[B + k * 64:B + k * 64 + 64]
        send_b[k, 64:72] = bias_tile
    for r in far8:
        send(send_b.at[(y + r) % NY], r1b.at[y], "b 1", yp(r))
    product(c, 1, acc)
    arrived(("half", 1))
    acc[1280:2560] += core_recv[1280:2560]
    for r in far4:
        send(rows(acc, A2 + (x + r) % NX * 192, 192), r1a2.at[r - 1], "a2 1", xp(r))
    for r in far8:
        send(rows(acc, C + (z + r) % NZ * 64, 64), r1c.at[r - 1], "c 1", zp(r))
    r1b[y] = send_b[y]

    enc_acc[...] = jnp.zeros_like(enc_acc)

    def pre(g, _):
        first = pl.multiple_of(g * ROWS, 128)
        gj = lax.dot_general(
            grad[pl.ds(first, ROWS)], w_ref[...], (((1,), (1,)), ((), ())), preferred_element_type=F32
        )
        j = joint[pl.ds(first, ROWS)].astype(F32)
        gp = gj * (1.0 - j * j)
        enc_acc[0:FR] += (gp[0:FR] + gp[FR:2 * FR]) + (gp[2 * FR:3 * FR] + gp[3 * FR:4 * FR])
        for k in range(GU):
            pred_acc[pl.ds(g * GU + k, 1), 0:H] = jnp.sum(gp[k * FR:(k + 1) * FR], axis=0, keepdims=True)
        return 0

    pred_acc[...] = jnp.zeros_like(pred_acc)
    lax.fori_loop(0, LB // GU, pre, 0)
    for k in range(5):
        enc_t[k * 128:(k + 1) * 128] = jnp.transpose(enc_acc[:, k * 128:(k + 1) * 128])

    def piece(r):
        return rows(enc_t, (z + r) % NZ * 80, 80)

    send(piece(4), e_up.at[0], "e up 0", zp(1))
    wide = pred_acc[...]
    for cc in range(2):
        for xx in range(4):
            for yy in range(4):
                start = (xx * 8 + yy * 2 + cc) * 20
                lo = start // 128 * 128
                two = wide[:, lo:lo + 256]
                pbuf[cc, xx, yy] = pltpu.roll(two, (256 - (start - lo)) % 256, 1)[:, 0:128]
    send(pbuf.at[other], p1_recv, "p 1", sibling)

    arrived("a1 1")
    s1a1[...] = (rows(acc, A1 + x * 192, 192)[...] + r1a1[0]) + (r1a1[1] + r1a1[2])
    for r in far8:
        send(rows(s1a1, (y + r) % NY * 24, 24), r2a1.at[r - 1], "a1 2", yp(r))
    arrived("b 1")
    sum_b = r1b[0]
    for k in range(1, NY):
        sum_b = sum_b + r1b[k]
    for k in range(NZ):
        s2b[k, 0:8] = sum_b[k * 8:k * 8 + 8]
        s2b[k, 8:16] = sum_b[64:72]
    for r in far8:
        send(s2b.at[(z + r) % NZ], r2b.at[z], "b 2", zp(r))
    arrived("a2 1")
    s1a2[...] = (rows(acc, A2 + x * 192, 192)[...] + r1a2[0]) + (r1a2[1] + r1a2[2])
    for r in far8:
        send(rows(s1a2, (z + r) % NZ * 24, 24), r2a2.at[r - 1], "a2 2", zp(r))
    arrived("c 1")
    sum_c = rows(acc, C + z * 64, 64)[...]
    for k in range(7):
        sum_c = sum_c + r1c[k]
    s1c[...] = sum_c
    for r in far8:
        send(rows(s1c, (y + r) % NY * 8, 8), r2c.at[r - 1], "c 2", yp(r))
    r2b[z] = s2b[z]

    arrived("e up 0")
    e_up[0] += piece(3)[...]
    send(e_up.at[0], e_up.at[1], "e up 1", zp(1))
    send(piece(5), e_down.at[0], "e down 0", zp(7))
    arrived("p 1")
    pbuf[c] = pbuf[c] + p1_recv[...]
    for r in far4:
        send(pbuf.at[c, (x + r) % NX], p2_recv.at[r - 1], "p 2", xp(r))

    arrived("b 2")
    sum_b = r2b[0]
    for k in range(1, NZ):
        sum_b = sum_b + r2b[k]
    r3b[x] = sum_b
    for r in far4:
        send(r3b.at[x], r3b.at[x], "b 3", xp(r))
    arrived("a1 2")
    sum_a = rows(s1a1, y * 24, 24)[...]
    for k in range(7):
        sum_a = sum_a + r2a1[k]
    r3a1[z] = sum_a
    for r in far8:
        send(r3a1.at[z], r3a1.at[z], "a1 3", zp(r))
    arrived("a2 2")
    sum_a = rows(s1a2, z * 24, 24)[...]
    for k in range(7):
        sum_a = sum_a + r2a2[k]
    r3a2[y] = sum_a
    for r in far8:
        send(r3a2.at[y], r3a2.at[y], "a2 3", yp(r))
    arrived("c 2")
    sum_c = rows(s1c, y * 8, 8)[...]
    for k in range(7):
        sum_c = sum_c + r2c[k]
    r3c[x] = sum_c
    for r in far4:
        send(r3c.at[x], r3c.at[x], "c 3", xp(r))

    arrived("e up 1")
    e_up[1] += piece(2)[...]
    send(e_up.at[1], e_up.at[2], "e up 2", zp(1))
    arrived("e down 0")
    e_down[0] += piece(6)[...]
    send(e_down.at[0], e_down.at[1], "e down 1", zp(7))
    arrived("p 2")
    pbuf[c, x] = (pbuf[c, x] + p2_recv[0]) + (p2_recv[1] + p2_recv[2])
    for r in far4:
        to = (ylo + r) % 4
        send(pbuf.at[c, x, to], p3_recv.at[r - 1], "p 3", place(x, yhi * 4 + to, z, c))

    base = c * HALF

    def spread(start, size, kind, peer, order, apart=False):
        part = rows(out_ref, base + start, size)
        for r in order:
            send(part, part, (kind, r) if apart else kind, peer(r))

    def across(start, size):
        part = rows(out_ref, base + start, size)
        send(part, part, "core", sibling)

    arrived("b 3")
    sum_b = (r3b[0] + r3b[1]) + (r3b[2] + r3b[3])
    rows(out_ref, base + B + (y * 8 + z) * 8, 8)[...] = sum_b[0:8]
    bias_out[...] = sum_b[8:16]
    spread(B + (y * 8 + z) * 8, 8, "b z", zp, far8)
    arrived("a1 3")
    sum_a = r3a1[0]
    for k in range(1, NZ):
        sum_a = sum_a + r3a1[k]
    rows(out_ref, base + A1 + (x * 8 + y) * 24, 24)[...] = sum_a
    spread(A1 + (x * 8 + y) * 24, 24, "a1 y", yp, far8, True)
    spread(A1 + (x * 8 + y) * 24, 24, "a1 x", xp, far4, True)
    arrived("a2 3")
    sum_a = r3a2[0]
    for k in range(1, NY):
        sum_a = sum_a + r3a2[k]
    rows(out_ref, base + A2 + (x * 8 + z) * 24, 24)[...] = sum_a
    spread(A2 + (x * 8 + z) * 24, 24, "a2 z", zp, far8, True)
    spread(A2 + (x * 8 + z) * 24, 24, "a2 x", xp, far4, True)
    arrived("c 3")
    rows(out_ref, base + C + (z * 8 + y) * 8, 8)[...] = (r3c[0] + r3c[1]) + (r3c[2] + r3c[3])
    spread(C + (z * 8 + y) * 8, 8, "c y", yp, far8)

    arrived("e up 2")
    e_up[2] += piece(1)[...]
    send(e_up.at[2], e_up.at[3], "e up 3", zp(1))
    arrived("e down 1")
    e_down[1] += piece(7)[...]
    send(e_down.at[1], e_down.at[2], "e down 2", zp(7))

    for n, r in enumerate(near8):
        arrived(("a1 y", r))
        spread(A1 + (x * 8 + (y + NY - r) % NY) * 24, 24, "a1 x", xp, far4, True)
        arrived(("a2 z", r))
        spread(A2 + (x * 8 + (z + NZ - r) % NZ) * 24, 24, "a2 x", xp, far4, True)
        if n == 3:
            arrived("b z")
            spread(B + y * 64, 64, "b y", yp, far8, True)
            arrived("c y")
            spread(C + z * 64, 64, "c z", zp, far8, True)
    across(A1 + x * 192, 192)
    across(A2 + x * 192, 192)
    across(B + y * 64, 64)
    across(C + z * 64, 64)

    arrived("e up 3")
    arrived("e down 2")
    e_sum[...] = piece(0)[...] + (e_up[3] + e_down[2])
    send(rows(e_sum, (1 - yhi) * 40, 40), e_last, "e y", yp(4))
    arrived("p 3")
    pred_out[...] = ((pbuf[c, x, ylo] + p3_recv[0]) + (p3_recv[1] + p3_recv[2]))[:, 0:20]

    for r in near8:
        arrived(("b y", r))
        across(B + (y + NY - r) % NY * 64, 64)
        arrived(("c z", r))
        across(C + (z + NZ - r) % NZ * 64, 64)
    for r in near4:
        arrived(("a1 x", r))
        across(A1 + (x + NX - r) % NX * 192, 192)
        arrived(("a2 x", r))
        across(A2 + (x + NX - r) % NX * 192, 192)
    arrived("e y")
    enc_out[...] = (rows(e_sum, yhi * 40, 40)[...] + e_last[...])[:, 0:FR]
    arrived("core")

    for kind in index:
        wait(ssem, kind)


def finish(weight, bias, enc, pred, weight_out, bias_out, enc_out, pred_out, sem):
    copies = [
        pltpu.make_async_copy(rows(weight, k * H, H), weight_out.at[:, pl.ds(k * 128, 128)], sem.at[k])
        for k in range(8)
    ]
    copies += [
        pltpu.make_async_copy(src, dst, sem.at[8 + k])
        for k, (src, dst) in enumerate(((bias, bias_out), (enc, enc_out), (pred, pred_out)))
    ]
    for copy in copies:
        copy.start()
    for copy in copies:
        copy.wait()


def vm(*shape, dtype=F32):
    return pltpu.VMEM(shape, dtype)


def local(encoder_out, predictor_out, out_weight, out_bias, target_labels, lengths, alpha, beta, log_likelihood):
    vmem = pl.BlockSpec(memory_space=pltpu.VMEM)
    hbm = pl.BlockSpec(memory_space=pltpu.HBM)
    sums = pl.pallas_call(
        kernel,
        out_shape=(vm(2 * HALF, 128), vm(8, 128), vm(40, FR), vm(LB, 20)),
        in_specs=[hbm] * 8 + [pl.BlockSpec(memory_space=pltpu.SMEM)],
        out_specs=(vmem, vmem, vmem, vmem),
        scratch_shapes=[
            vm(FR, H, dtype=BF16), vm(LB, H, dtype=BF16), vm(H, V, dtype=BF16), vm(1, V),
            pltpu.SMEM((LB,), jnp.int32), pltpu.SMEM((2,), jnp.int32), vm(LB, FR), vm(LB, FR),
            pltpu.SemaphoreType.DMA((8,)),
            vm(FR, H), vm(LB, H), vm(FR * LB, H, dtype=BF16), vm(FR * LB, V), vm(FR * LB, V, dtype=BF16),
            vm(LB, 128), vm(LB, 128), vm(8, 128), vm(3, 128, 128), vm(FR, 128), vm(FR, 128), vm(FR, 128),
            vm(FR, 128), vm(FR, 128),
            vm(8, V), vm(HALF + 8, 128), vm(HALF + 8, 128), vm(HALF + 8, 128), vm(8, 72, 128),
            vm(3, 192, 128), vm(8, 72, 128), vm(3, 192, 128), vm(7, 64, 128),
            vm(192, 128), vm(192, 128), vm(64, 128), vm(8, 16, 128),
            vm(7, 24, 128), vm(8, 16, 128), vm(7, 24, 128), vm(7, 8, 128),
            vm(8, 24, 128), vm(4, 16, 128), vm(8, 24, 128), vm(4, 8, 128),
            vm(128, H), vm(H, 128), vm(4, 80, 128), vm(3, 80, 128), vm(80, 128), vm(40, 128),
            vm(LB, 768), vm(2, 4, 4, LB, 128), vm(4, 4, LB, 128), vm(3, 4, LB, 128), vm(3, LB, 128),
            pltpu.SemaphoreType.DMA((SEMS,)), pltpu.SemaphoreType.DMA((SEMS,)),
        ],
        compiler_params=pltpu.CompilerParams(
            collective_id=0, has_side_effects=True, vmem_limit_bytes=44 * 2**20
        ),
        name="joint_backward",
    )(*(
        pltpu.with_memory_space_constraint(a, pltpu.HBM) for a in (
            encoder_out, predictor_out, out_weight, out_bias.reshape(1, V), target_labels, lengths, alpha.T, beta.T,
        )
    ), log_likelihood)
    weight, bias, enc, pred = pl.pallas_call(
        finish,
        out_shape=(
            jax.ShapeDtypeStruct((H, V), F32),
            jax.ShapeDtypeStruct((8, 128), F32),
            jax.ShapeDtypeStruct((40, FR), F32),
            jax.ShapeDtypeStruct((LB, 20), F32),
        ),
        in_specs=[pl.BlockSpec(memory_space=pl.ANY)] * 4,
        out_specs=[hbm] * 4,
        scratch_shapes=[pltpu.SemaphoreType.DMA((11,))],
        compiler_params=pltpu.CompilerParams(vmem_limit_bytes=2 * 2**20),
        name="finish",
    )(*sums)
    return enc.T, pred, weight, bias.reshape(V)


def solution(mesh):
    placed = (
        P("frames", None), P("labels", None), P(), P(), P("labels"), P(),
        P("frames", "labels"), P("frames", "labels"), P(),
    )
    return jax.shard_map(
        local,
        mesh=mesh,
        in_specs=placed,
        out_specs=(P("frames", "labels"), P("labels", "frames"), P(), P()),
        check_vma=False,
    )
```

time: 83.8 us -> 67.3 us (0.80)
  local copies, waits for them, and re-layouts: 9.09 us -> 0 us
  Pallas kernels: 73.1 us -> 65.9 us
    pallas_call x1 -> x2, Pallas kernels: 73.1 us -> 65.9 us  [the longest x1 64.3 us: local(): pl.pallas_call(kernel, out_shape=(vm(2 * HALF, 128), vm(8, 128), vm(40, F...]
    unnamed x9 -> x0, local copies, waits for them, and re-layouts: 5.49 us -> none
    reshape x1 -> x0, local copies, waits for them, and re-layouts: 3.6 us -> none  [local(): grad_weight = weight.reshape(8, H, 128).transpose(1, 0, 2).reshape(H, V)]
where the time goes in v2:
time: 67.3 us; the launch traced here: 67.2 us
  Pallas kernels  65.9 us (98%)
  between operations  1.29 us (2%)
    pallas_call x1, Pallas kernels, local(): pl.pallas_call(kernel, out_shape=(vm(2 * HALF, 128), vm(8, 128), vm(40, F...  64.3 us
    pallas_call x1, Pallas kernels, local(): pl.pallas_call(finish, out_shape=(jax.ShapeDtypeStruct((H, V), F32), jax....  1.58 us

profile of v2, /device:TPU:1, one launch (start us, length us, event | category | flops | bytes accessed | tf_op | source)
XLA Modules:
  0.0 67.2 jit_solution(16745353801530365696)
XLA Ops:
  1.3 64.3 %joint_backward.1 = (f32[5120,128]{1,0:T(8,128)S(1)}, f32[8,128]{1,0:T(8,128)S(1)}, f32[40,96]{1,0:T(8,128)S(1)}, f32[16,20]{1,0:T(8,128)S(1)}) custom-call(bf16[96,640]{1,0:T(8,128)(2,1)} %enc_in.1, bf16[16,640]{1,0:T(8,128)(2,1)} %pred_in.1, bf16[640,1024]{1,0:T(8,128)(2,1)} %w_in.1, f32[1,1024]{1,0:T(1,128)} %bitcast.7, s32[16]{0:T(128)} %labels_in.1, ...), custom_call_target="tpu_custom_call" | custom-call | tf_op jit(solution)/shard_map/joint_backward/pallas_call | solution.py:432
  65.6 1.6 %finish.1 = (f32[640,1024]{1,0:T(8,128)}, f32[8,128]{1,0:T(8,128)}, f32[40,96]{1,0:T(8,128)}, f32[16,20]{1,0:T(8,128)}) custom-call(f32[5120,128]{1,0:T(8,128)S(1)} %get-tuple-element.12.weight, f32[8,128]{1,0:T(8,128)S(1)} %get-tuple-element.13.bias, f32[40,96]{1,0:T(8,128)S(1)} %get-tuple-element.14.enc, f32[16,20]{1,0:T(8,128)S(1)} %get-tuple-element.15.pred), custom_call_target="tpu_custom_call" | custom-call | tf_op jit(solution)/shard_map/finish/pallas_call | solution.py:462

commit v3 on v2

--- a/solution.py
+++ b/solution.py
@@ -28,7 +28,7 @@
     enc_in, pred_in, w_in, bias_in, labels_in, lengths_in, alpha_in, beta_in, ll_ref,
     out_ref, bias_out, enc_out, pred_out,
     enc_ref, pred_ref, w_ref, bias_ref, labels_ref, lengths_ref, alpha_ref, beta_ref, isem,
-    encf, predf, joint, expo, grad, bsend, brow, bcol, turn, ssum, slab, sblank, occb, occl,
+    encf, predf, joint, expo, grad, bsend, brow, bcol, turn, alpha_t, total, ssum, slab, sblank, occb, occl,
     bias_acc, peer_half, core_recv, acc, send_b,
     r1a1, r1b, r1a2, r1c, s1a1, s1a2, s1c, s2b, r2a1, r2b, r2a2, r2c,
     r3a1, r3b, r3a2, r3c,
@@ -73,11 +73,19 @@
     def arrived(kind):
         wait(rsem, kind)
 
+    gone = set()
+
+    def drain(kinds):
+        for kind in kinds:
+            if kind not in gone:
+                gone.add(kind)
+                wait(ssem, kind)
+
     loads = [
         pltpu.make_async_copy(src, dst, isem.at[k])
         for k, (src, dst) in enumerate((
-            (enc_in, enc_ref), (pred_in, pred_ref), (beta_in, beta_ref), (alpha_in, alpha_ref), (bias_in, bias_ref),
-            (labels_in, labels_ref), (lengths_in, lengths_ref), (w_in, w_ref),
+            (enc_in, enc_ref), (pred_in, pred_ref), (w_in, w_ref), (beta_in, beta_ref), (alpha_in, alpha_ref),
+            (bias_in, bias_ref), (labels_in, labels_ref), (lengths_in, lengths_ref),
         ))
     ]
     for load in loads:
@@ -90,94 +98,106 @@
     for p in peers:
         pl.semaphore_signal(barrier, inc=1, device_id=p, device_id_type=MESH)
 
-    for load in loads:
-        load.wait()
-
-    encf[...] = enc_ref[...].astype(F32)
-    predf[...] = pred_ref[...].astype(F32)
-    bsend[...] = jnp.zeros_like(bsend)
-    bsend[:, 0:FR] = beta_ref[...]
-    turn[...] = jnp.zeros_like(turn)
-    turn[0, 0:LB, 0:FR] = alpha_ref[...]
-    ssum[...] = jnp.ones_like(ssum)
-    slab[...] = jnp.zeros_like(slab)
-    sblank[...] = jnp.zeros_like(sblank)
     lane = lax.broadcasted_iota(jnp.int32, (1, 128), 1)
     vocab = lax.broadcasted_iota(jnp.int32, (1, V), 1)
 
-    def forward(g, _):
+    def squash(g):
         for k in range(GU):
             u = g * GU + k
-            start = pl.multiple_of(u * FR, 32)
-            joint[pl.ds(start, FR)] = jnp.tanh(encf[...] + predf[pl.ds(u, 1)]).astype(BF16)
-        first = pl.multiple_of(g * ROWS, 128)
-        logits = jnp.dot(joint[pl.ds(first, ROWS)], w_ref[...], preferred_element_type=F32) + bias_ref[...]
+            joint[u * FR:(u + 1) * FR] = jnp.tanh(encf[...] + predf[u:u + 1]).astype(BF16)
+
+    def forward(g):
+        logits = jnp.dot(joint[g * ROWS:(g + 1) * ROWS], w_ref[...], preferred_element_type=F32) + bias_ref[...]
         for k in range(GU):
             u = g * GU + k
-            start = pl.multiple_of(u * FR, 32)
             part = logits[k * FR:(k + 1) * FR]
             e = jnp.exp(part)
-            expo[pl.ds(start, FR)] = e
+            expo[u * FR:(u + 1) * FR] = e
             hot = vocab == labels_ref[u]
             here = lane == u
             ssum[...] = jnp.where(here, jnp.sum(e, axis=1, keepdims=True), ssum[...])
             slab[...] = jnp.where(here, jnp.sum(jnp.where(hot, part, 0.0), axis=1, keepdims=True), slab[...])
             sblank[...] = jnp.where(here, part[:, 0:1], sblank[...])
-        return 0
-
-    forward(0, 0)
+
+    loads[0].wait()
+    loads[1].wait()
+    encf[...] = enc_ref[...].astype(F32)
+    predf[...] = pred_ref[...].astype(F32)
+    ssum[...] = jnp.ones_like(ssum)
+    slab[...] = jnp.zeros_like(slab)
+    sblank[...] = jnp.zeros_like(sblank)
+    squash(0)
+    for load in loads[2:]:
+        load.wait()
+    bsend[...] = jnp.zeros_like(bsend)
+    bsend[:, 0:FR] = beta_ref[...]
+    turn[...] = jnp.zeros_like(turn)
+    turn[0, 0:LB, 0:FR] = alpha_ref[...]
+    squash(1)
+    forward(0)
     pl.semaphore_wait(barrier, len(peers))
     send(bsend, brow, "frame", ((f + 31) % 32, l))
     send(bsend.at[pl.ds(0, 8)], bcol, "label", (f, (l + 15) % 16))
-    lax.fori_loop(1, LB // GU, forward, 0)
-
-    arrived("frame")
-    arrived("label")
+    squash(2)
+    forward(1)
+    squash(3)
+    forward(2)
+    forward(3)
+
     frame_len, label_len, log_total = lengths_ref[0], lengths_ref[1], ll_ref[0]
-    beta = bsend[...]
     label_row = lax.broadcasted_iota(jnp.int32, (LB, 128), 0)
-    turn[1, 0:LB] = jnp.where(lane == FR - 1, brow[:, 0:1], pltpu.roll(beta, 127, 1))
-    turn[2, 0:LB] = jnp.where(label_row == LB - 1, bcol[0:1, :], pltpu.roll(beta, LB - 1, 0))
-    alpha = jnp.transpose(turn[0])[0:FR]
-    beta_frame = jnp.transpose(turn[1])[0:FR]
-    beta_label = jnp.transpose(turn[2])[0:FR]
     t_pos = lax.broadcasted_iota(jnp.int32, (FR, 128), 0) + f * FR
     u_here = lax.broadcasted_iota(jnp.int32, (FR, 128), 1)
     u_pos = u_here + l * LB
-    total = ssum[...]
-    lse = jnp.log(total)
-    inner = (t_pos < frame_len - 1) & (u_pos <= label_len)
-    final = (t_pos == frame_len - 1) & (u_pos == label_len)
-    blank_ok = (inner | final) & (u_here < LB)
-    blank_arg = alpha + (sblank[...] - lse) + jnp.where(inner, beta_frame, 0.0) - log_total
-    occb[...] = jnp.where(blank_ok, jnp.exp(jnp.where(blank_ok, blank_arg, 0.0)), 0.0)
-    label_ok = (t_pos < frame_len) & (u_pos < label_len) & (u_here < LB)
-    label_arg = alpha + (slab[...] - lse) + beta_label - log_total
-    occl[...] = jnp.where(label_ok, jnp.exp(jnp.where(label_ok, label_arg, 0.0)), 0.0)
-    ssum[...] = 4.0 / total
+    total[...] = ssum[...]
+    ssum[...] = 4.0 / total[...]
+    alpha_t[...] = jnp.transpose(turn[0])[0:FR]
+
+    def occupancies(next_frame, next_label):
+        turn[1, 0:LB] = next_frame
+        turn[2, 0:LB] = next_label
+        alpha = alpha_t[...]
+        beta_frame = jnp.transpose(turn[1])[0:FR]
+        beta_label = jnp.transpose(turn[2])[0:FR]
+        lse = jnp.log(total[...])
+        inner = (t_pos < frame_len - 1) & (u_pos <= label_len)
+        final = (t_pos == frame_len - 1) & (u_pos == label_len)
+        blank_ok = (inner | final) & (u_here < LB)
+        blank_arg = alpha + (sblank[...] - lse) + jnp.where(inner, beta_frame, 0.0) - log_total
+        occb[...] = jnp.where(blank_ok, jnp.exp(jnp.where(blank_ok, blank_arg, 0.0)), 0.0)
+        label_ok = (t_pos < frame_len) & (u_pos < label_len) & (u_here < LB)
+        label_arg = alpha + (slab[...] - lse) + beta_label - log_total
+        occl[...] = jnp.where(label_ok, jnp.exp(jnp.where(label_ok, label_arg, 0.0)), 0.0)
 
     bias_acc[...] = jnp.zeros_like(bias_acc)
 
-    def backward(u, _):
-        here = lane == u
-        start = pl.multiple_of(u * FR, 32)
-
-        def column(ref):
-            return jnp.sum(jnp.where(here, ref[...], 0.0), axis=1, keepdims=True)
-
-        blank, label, inverse = column(occb), column(occl), column(ssum)
+    def backward(u, low, count):
+        start = u * FR + low
+        blank, label, inverse = (ref[low:low + count, u:u + 1] for ref in (occb, occl, ssum))
         quarter = (blank + label) * 0.25
         hot = vocab == labels_ref[u]
-        g = (expo[pl.ds(start, FR)] * inverse) * quarter
+        g = (expo[start:start + count] * inverse) * quarter
         g = jnp.where(hot, g - label, g)
         g0 = jnp.where(lane == 0, g[:, 0:128] - blank, g[:, 0:128])
-        grad[pl.ds(start, FR)] = g.astype(BF16)
-        grad[pl.ds(start, FR), 0:128] = g0.astype(BF16)
-        bias_acc[:, 128:] += jnp.sum(g[:, 128:].reshape(FR // 8, 8, V - 128), axis=0)
-        bias_acc[:, 0:128] += jnp.sum(g0.reshape(FR // 8, 8, 128), axis=0)
-        return 0
-
-    lax.fori_loop(0, LB, backward, 0)
+        grad[start:start + count, 128:] = g[:, 128:].astype(BF16)
+        grad[start:start + count, 0:128] = g0.astype(BF16)
+        bias_acc[:, 128:] += jnp.sum(g[:, 128:].reshape(count // 8, 8, V - 128), axis=0)
+        bias_acc[:, 0:128] += jnp.sum(g0.reshape(count // 8, 8, 128), axis=0)
+
+    beta = bsend[...]
+    frame_shift, label_shift = pltpu.roll(beta, 127, 1), pltpu.roll(beta, LB - 1, 0)
+    occupancies(frame_shift, label_shift)
+    for u in range(LB - 1):
+        backward(u, 0, FR - 16)
+    arrived("frame")
+    arrived("label")
+    occupancies(
+        jnp.where(lane == FR - 1, brow[:, 0:1], frame_shift),
+        jnp.where(label_row == LB - 1, bcol[0:1, :], label_shift),
+    )
+    for u in range(LB - 1):
+        backward(u, FR - 16, 16)
+    backward(LB - 1, 0, FR)
 
     def product(half, q, ref):
         base = pl.multiple_of(half * 512 + q * 256, 256)
@@ -194,14 +214,17 @@
                 peer_half[HALF + k:HALF + k + 1] = jnp.sum(bias_acc[:, k * 128:(k + 1) * 128], axis=0, keepdims=True)
             acc[HALF:HALF + 8] = peer_half[HALF:HALF + 8]
             send(rows(peer_half, HALF, 8), rows(core_recv, HALF, 8), "bias", sibling)
-        send(rows(peer_half, q * 1280, 1280), rows(core_recv, q * 1280, 1280), ("half", q), sibling)
+        for start, size in ((0, 768), (768, 512)):
+            part = q * 1280 + start
+            send(rows(peer_half, part, size), rows(core_recv, part, size), ("half", part), sibling)
     product(c, 0, acc)
 
-    arrived("bias")
-    arrived(("half", 0))
+    arrived(("half", A1))
     acc[0:768] += core_recv[0:768]
     for r in far4:
         send(rows(acc, A1 + (x + r) % NX * 192, 192), r1a1.at[r - 1], "a1 1", xp(r))
+    arrived("bias")
+    arrived(("half", B))
     bias_tile = acc[HALF:HALF + 8] + core_recv[HALF:HALF + 8]
     for k in range(NY):
         send_b[k, 0:64] = acc[B + k * 64:B + k * 64 + 64] + core_recv[B + k * 64:B + k * 64 + 64]
@@ -209,10 +232,12 @@
     for r in far8:
         send(send_b.at[(y + r) % NY], r1b.at[y], "b 1", yp(r))
     product(c, 1, acc)
-    arrived(("half", 1))
-    acc[1280:2560] += core_recv[1280:2560]
+    arrived(("half", A2))
+    acc[A2:C] += core_recv[A2:C]
     for r in far4:
         send(rows(acc, A2 + (x + r) % NX * 192, 192), r1a2.at[r - 1], "a2 1", xp(r))
+    arrived(("half", C))
+    acc[C:HALF] += core_recv[C:HALF]
     for r in far8:
         send(rows(acc, C + (z + r) % NZ * 64, 64), r1c.at[r - 1], "c 1", zp(r))
     r1b[y] = send_b[y]
@@ -250,6 +275,11 @@
                 pbuf[cc, xx, yy] = pltpu.roll(two, (256 - (start - lo)) % 256, 1)[:, 0:128]
     send(pbuf.at[other], p1_recv, "p 1", sibling)
 
+    arrived("e up 0")
+    e_up[0] += piece(3)[...]
+    send(e_up.at[0], e_up.at[1], "e up 1", zp(1))
+    send(piece(5), e_down.at[0], "e down 0", zp(7))
+
     arrived("a1 1")
     s1a1[...] = (rows(acc, A1 + x * 192, 192)[...] + r1a1[0]) + (r1a1[1] + r1a1[2])
     for r in far8:
@@ -276,14 +306,18 @@
         send(rows(s1c, (y + r) % NY * 8, 8), r2c.at[r - 1], "c 2", yp(r))
     r2b[z] = s2b[z]
 
-    arrived("e up 0")
-    e_up[0] += piece(3)[...]
-    send(e_up.at[0], e_up.at[1], "e up 1", zp(1))
-    send(piece(5), e_down.at[0], "e down 0", zp(7))
+    arrived("e up 1")
+    e_up[1] += piece(2)[...]
+    send(e_up.at[1], e_up.at[2], "e up 2", zp(1))
+    arrived("e down 0")
+    e_down[0] += piece(6)[...]
+    send(e_down.at[0], e_down.at[1], "e down 1", zp(7))
     arrived("p 1")
     pbuf[c] = pbuf[c] + p1_recv[...]
     for r in far4:
         send(pbuf.at[c, (x + r) % NX], p2_recv.at[r - 1], "p 2", xp(r))
+
+    before = list(index)
 
     arrived("b 2")
     sum_b = r2b[0]
@@ -314,12 +348,12 @@
     for r in far4:
         send(r3c.at[x], r3c.at[x], "c 3", xp(r))
 
-    arrived("e up 1")
-    e_up[1] += piece(2)[...]
-    send(e_up.at[1], e_up.at[2], "e up 2", zp(1))
-    arrived("e down 0")
-    e_down[0] += piece(6)[...]
-    send(e_down.at[0], e_down.at[1], "e down 1", zp(7))
+    arrived("e up 2")
+    e_up[2] += piece(1)[...]
+    send(e_up.at[2], e_up.at[3], "e up 3", zp(1))
+    arrived("e down 1")
+    e_down[1] += piece(7)[...]
+    send(e_down.at[1], e_down.at[2], "e down 2", zp(7))
     arrived("p 2")
     pbuf[c, x] = (pbuf[c, x] + p2_recv[0]) + (p2_recv[1] + p2_recv[2])
     for r in far4:
@@ -360,12 +394,11 @@
     rows(out_ref, base + C + (z * 8 + y) * 8, 8)[...] = (r3c[0] + r3c[1]) + (r3c[2] + r3c[3])
     spread(C + (z * 8 + y) * 8, 8, "c y", yp, far8)
 
-    arrived("e up 2")
-    e_up[2] += piece(1)[...]
-    send(e_up.at[2], e_up.at[3], "e up 3", zp(1))
-    arrived("e down 1")
-    e_down[1] += piece(7)[...]
-    send(e_down.at[1], e_down.at[2], "e down 2", zp(7))
+    arrived("e up 3")
+    arrived("e down 2")
+    e_sum[...] = piece(0)[...] + (e_up[3] + e_down[2])
+    send(rows(e_sum, (1 - yhi) * 40, 40), e_last, "e y", yp(4))
+    drain(before)
 
     for n, r in enumerate(near8):
         arrived(("a1 y", r))
@@ -382,10 +415,6 @@
     across(B + y * 64, 64)
     across(C + z * 64, 64)
 
-    arrived("e up 3")
-    arrived("e down 2")
-    e_sum[...] = piece(0)[...] + (e_up[3] + e_down[2])
-    send(rows(e_sum, (1 - yhi) * 40, 40), e_last, "e y", yp(4))
     arrived("p 3")
     pred_out[...] = ((pbuf[c, x, ylo] + p3_recv[0]) + (p3_recv[1] + p3_recv[2]))[:, 0:20]
 
@@ -403,8 +432,7 @@
     enc_out[...] = (rows(e_sum, yhi * 40, 40)[...] + e_last[...])[:, 0:FR]
     arrived("core")
 
-    for kind in index:
-        wait(ssem, kind)
+    drain(list(index))
 
 
 def finish(weight, bias, enc, pred, weight_out, bias_out, enc_out, pred_out, sem):
@@ -439,7 +467,7 @@
             pltpu.SMEM((LB,), jnp.int32), pltpu.SMEM((2,), jnp.int32), vm(LB, FR), vm(LB, FR),
             pltpu.SemaphoreType.DMA((8,)),
             vm(FR, H), vm(LB, H), vm(FR * LB, H, dtype=BF16), vm(FR * LB, V), vm(FR * LB, V, dtype=BF16),
-            vm(LB, 128), vm(LB, 128), vm(8, 128), vm(3, 128, 128), vm(FR, 128), vm(FR, 128), vm(FR, 128),
+            vm(LB, 128), vm(LB, 128), vm(8, 128), vm(3, 128, 128), vm(FR, 128), vm(FR, 128), vm(FR, 128), vm(FR, 128), vm(FR, 128),
             vm(FR, 128), vm(FR, 128),
             vm(8, V), vm(HALF + 8, 128), vm(HALF + 8, 128), vm(HALF + 8, 128), vm(8, 72, 128),
             vm(3, 192, 128), vm(8, 72, 128), vm(3, 192, 128), vm(7, 64, 128),

time: 67.3 us -> 64.7 us (0.961)
  Pallas kernels: 65.9 us -> 63.3 us
    pallas_call x1, Pallas kernels: 64.3 us -> 61.7 us  [local(): pl.pallas_call(kernel, out_shape=(vm(2 * HALF, 128), vm(8, 128), vm(40, F...]
where the time goes in v3:
time: 64.7 us; the launch traced here: 64.6 us
  Pallas kernels  63.3 us (98%)
  between operations  1.29 us (2%)
    pallas_call x1, Pallas kernels, local(): pl.pallas_call(kernel, out_shape=(vm(2 * HALF, 128), vm(8, 128), vm(40, F...  61.7 us
    pallas_call x1, Pallas kernels, local(): pl.pallas_call(finish, out_shape=(jax.ShapeDtypeStruct((H, V), F32), jax....  1.58 us

profile of v3, /device:TPU:1, one launch (start us, length us, event | category | flops | bytes accessed | tf_op | source)
XLA Modules:
  0.0 64.6 jit_solution(13986076816807144569)
XLA Ops:
  1.3 61.7 %joint_backward.1 = (f32[5120,128]{1,0:T(8,128)S(1)}, f32[8,128]{1,0:T(8,128)S(1)}, f32[40,96]{1,0:T(8,128)S(1)}, f32[16,20]{1,0:T(8,128)S(1)}) custom-call(bf16[96,640]{1,0:T(8,128)(2,1)} %enc_in.1, bf16[16,640]{1,0:T(8,128)(2,1)} %pred_in.1, bf16[640,1024]{1,0:T(8,128)(2,1)} %w_in.1, f32[1,1024]{1,0:T(1,128)} %bitcast.7, s32[16]{0:T(128)} %labels_in.1, ...), custom_call_target="tpu_custom_call" | custom-call | tf_op jit(solution)/shard_map/joint_backward/pallas_call | solution.py:460
  63.0 1.6 %finish.1 = (f32[640,1024]{1,0:T(8,128)}, f32[8,128]{1,0:T(8,128)}, f32[40,96]{1,0:T(8,128)}, f32[16,20]{1,0:T(8,128)}) custom-call(f32[5120,128]{1,0:T(8,128)S(1)} %get-tuple-element.12.weight, f32[8,128]{1,0:T(8,128)S(1)} %get-tuple-element.13.bias, f32[40,96]{1,0:T(8,128)S(1)} %get-tuple-element.14.enc, f32[16,20]{1,0:T(8,128)S(1)} %get-tuple-element.15.pred), custom_call_target="tpu_custom_call" | custom-call | tf_op jit(solution)/shard_map/finish/pallas_call | solution.py:490

commit v4 on v3

--- a/solution.py
+++ b/solution.py
@@ -275,11 +275,6 @@
                 pbuf[cc, xx, yy] = pltpu.roll(two, (256 - (start - lo)) % 256, 1)[:, 0:128]
     send(pbuf.at[other], p1_recv, "p 1", sibling)
 
-    arrived("e up 0")
-    e_up[0] += piece(3)[...]
-    send(e_up.at[0], e_up.at[1], "e up 1", zp(1))
-    send(piece(5), e_down.at[0], "e down 0", zp(7))
-
     arrived("a1 1")
     s1a1[...] = (rows(acc, A1 + x * 192, 192)[...] + r1a1[0]) + (r1a1[1] + r1a1[2])
     for r in far8:
@@ -288,51 +283,59 @@
     sum_b = r1b[0]
     for k in range(1, NY):
         sum_b = sum_b + r1b[k]
-    for k in range(NZ):
-        s2b[k, 0:8] = sum_b[k * 8:k * 8 + 8]
-        s2b[k, 8:16] = sum_b[64:72]
-    for r in far8:
-        send(s2b.at[(z + r) % NZ], r2b.at[z], "b 2", zp(r))
-    arrived("a2 1")
-    s1a2[...] = (rows(acc, A2 + x * 192, 192)[...] + r1a2[0]) + (r1a2[1] + r1a2[2])
-    for r in far8:
-        send(rows(s1a2, (z + r) % NZ * 24, 24), r2a2.at[r - 1], "a2 2", zp(r))
+    for k in range(NX):
+        s2b[k, 0:16] = sum_b[k * 16:k * 16 + 16]
+        s2b[k, 16:24] = sum_b[64:72]
+    for r in far4:
+        send(s2b.at[(x + r) % NX], r2b.at[x], "b 2", xp(r))
+    r2b[x] = s2b[x]
     arrived("c 1")
     sum_c = rows(acc, C + z * 64, 64)[...]
     for k in range(7):
         sum_c = sum_c + r1c[k]
     s1c[...] = sum_c
-    for r in far8:
-        send(rows(s1c, (y + r) % NY * 8, 8), r2c.at[r - 1], "c 2", yp(r))
-    r2b[z] = s2b[z]
-
+    for r in far4:
+        send(rows(s1c, (x + r) % NX * 16, 16), r2c.at[r - 1], "c 2", xp(r))
+    arrived("p 1")
+    pbuf[c] = pbuf[c] + p1_recv[...]
+    for r in far4:
+        send(pbuf.at[c, (x + r) % NX], p2_recv.at[r - 1], "p 2", xp(r))
+    arrived("e up 0")
+    e_up[0] += piece(3)[...]
+    arrived("a2 1")
+    s1a2[...] = (rows(acc, A2 + x * 192, 192)[...] + r1a2[0]) + (r1a2[1] + r1a2[2])
+    for r in far8:
+        send(rows(s1a2, (z + r) % NZ * 24, 24), r2a2.at[r - 1], "a2 2", zp(r))
+    send(e_up.at[0], e_up.at[1], "e up 1", zp(1))
+    send(piece(5), e_down.at[0], "e down 0", zp(7))
+    before = list(index)
+
+    arrived("b 2")
+    r3b[z] = (r2b[0] + r2b[1]) + (r2b[2] + r2b[3])
+    for r in far8:
+        send(r3b.at[z], r3b.at[z], "b 3", zp(r))
+    arrived("c 2")
+    r3c[y] = (rows(s1c, x * 16, 16)[...] + r2c[0]) + (r2c[1] + r2c[2])
+    for r in far8:
+        send(r3c.at[y], r3c.at[y], "c 3", yp(r))
+    arrived("a1 2")
+    sum_a = rows(s1a1, y * 24, 24)[...]
+    for k in range(7):
+        sum_a = sum_a + r2a1[k]
+    r3a1[z] = sum_a
+    for r in far8:
+        send(r3a1.at[z], r3a1.at[z], "a1 3", zp(r))
     arrived("e up 1")
     e_up[1] += piece(2)[...]
     send(e_up.at[1], e_up.at[2], "e up 2", zp(1))
     arrived("e down 0")
     e_down[0] += piece(6)[...]
     send(e_down.at[0], e_down.at[1], "e down 1", zp(7))
-    arrived("p 1")
-    pbuf[c] = pbuf[c] + p1_recv[...]
+    arrived("p 2")
+    pbuf[c, x] = (pbuf[c, x] + p2_recv[0]) + (p2_recv[1] + p2_recv[2])
     for r in far4:
-        send(pbuf.at[c, (x + r) % NX], p2_recv.at[r - 1], "p 2", xp(r))
-
-    before = list(index)
-
-    arrived("b 2")
-    sum_b = r2b[0]
-    for k in range(1, NZ):
-        sum_b = sum_b + r2b[k]
-    r3b[x] = sum_b
-    for r in far4:
-        send(r3b.at[x], r3b.at[x], "b 3", xp(r))
-    arrived("a1 2")
-    sum_a = rows(s1a1, y * 24, 24)[...]
-    for k in range(7):
-        sum_a = sum_a + r2a1[k]
-    r3a1[z] = sum_a
-    for r in far8:
-        send(r3a1.at[z], r3a1.at[z], "a1 3", zp(r))
+        to = (ylo + r) % 4
+        send(pbuf.at[c, x, to], p3_recv.at[r - 1], "p 3", place(x, yhi * 4 + to, z, c))
     arrived("a2 2")
     sum_a = rows(s1a2, z * 24, 24)[...]
     for k in range(7):
@@ -340,25 +343,6 @@
     r3a2[y] = sum_a
     for r in far8:
         send(r3a2.at[y], r3a2.at[y], "a2 3", yp(r))
-    arrived("c 2")
-    sum_c = rows(s1c, y * 8, 8)[...]
-    for k in range(7):
-        sum_c = sum_c + r2c[k]
-    r3c[x] = sum_c
-    for r in far4:
-        send(r3c.at[x], r3c.at[x], "c 3", xp(r))
-
-    arrived("e up 2")
-    e_up[2] += piece(1)[...]
-    send(e_up.at[2], e_up.at[3], "e up 3", zp(1))
-    arrived("e down 1")
-    e_down[1] += piece(7)[...]
-    send(e_down.at[1], e_down.at[2], "e down 2", zp(7))
-    arrived("p 2")
-    pbuf[c, x] = (pbuf[c, x] + p2_recv[0]) + (p2_recv[1] + p2_recv[2])
-    for r in far4:
-        to = (ylo + r) % 4
-        send(pbuf.at[c, x, to], p3_recv.at[r - 1], "p 3", place(x, yhi * 4 + to, z, c))
 
     base = c * HALF
 
@@ -372,10 +356,18 @@
         send(part, part, "core", sibling)
 
     arrived("b 3")
-    sum_b = (r3b[0] + r3b[1]) + (r3b[2] + r3b[3])
-    rows(out_ref, base + B + (y * 8 + z) * 8, 8)[...] = sum_b[0:8]
-    bias_out[...] = sum_b[8:16]
-    spread(B + (y * 8 + z) * 8, 8, "b z", zp, far8)
+    sum_b = r3b[0]
+    for k in range(1, NZ):
+        sum_b = sum_b + r3b[k]
+    rows(out_ref, base + B + (y * 4 + x) * 16, 16)[...] = sum_b[0:16]
+    bias_out[...] = sum_b[16:24]
+    spread(B + (y * 4 + x) * 16, 16, "b x", xp, far4)
+    arrived("c 3")
+    sum_c = r3c[0]
+    for k in range(1, NY):
+        sum_c = sum_c + r3c[k]
+    rows(out_ref, base + C + (z * 4 + x) * 16, 16)[...] = sum_c
+    spread(C + (z * 4 + x) * 16, 16, "c x", xp, far4)
     arrived("a1 3")
     sum_a = r3a1[0]
     for k in range(1, NZ):
@@ -383,6 +375,13 @@
     rows(out_ref, base + A1 + (x * 8 + y) * 24, 24)[...] = sum_a
     spread(A1 + (x * 8 + y) * 24, 24, "a1 y", yp, far8, True)
     spread(A1 + (x * 8 + y) * 24, 24, "a1 x", xp, far4, True)
+    arrived("e up 2")
+    e_up[2] += piece(1)[...]
+    send(e_up.at[2], e_up.at[3], "e up 3", zp(1))
+    arrived("e down 1")
+    e_down[1] += piece(7)[...]
+    send(e_down.at[1], e_down.at[2], "e down 2", zp(7))
+    drain(before)
     arrived("a2 3")
     sum_a = r3a2[0]
     for k in range(1, NY):
@@ -390,46 +389,47 @@
     rows(out_ref, base + A2 + (x * 8 + z) * 24, 24)[...] = sum_a
     spread(A2 + (x * 8 + z) * 24, 24, "a2 z", zp, far8, True)
     spread(A2 + (x * 8 + z) * 24, 24, "a2 x", xp, far4, True)
-    arrived("c 3")
-    rows(out_ref, base + C + (z * 8 + y) * 8, 8)[...] = (r3c[0] + r3c[1]) + (r3c[2] + r3c[3])
-    spread(C + (z * 8 + y) * 8, 8, "c y", yp, far8)
-
+
+    def pass_a1(r):
+        arrived(("a1 y", r))
+        spread(A1 + (x * 8 + (y + NY - r) % NY) * 24, 24, "a1 x", xp, far4, True)
+
+    def pass_a2(r):
+        arrived(("a2 z", r))
+        spread(A2 + (x * 8 + (z + NZ - r) % NZ) * 24, 24, "a2 x", xp, far4, True)
+
+    arrived("b x")
+    spread(B + y * 64, 64, "b y", yp, far8, True)
+    arrived("c x")
+    spread(C + z * 64, 64, "c z", zp, far8, True)
+    for r in near8:
+        pass_a1(r)
+    across(A1 + x * 192, 192)
+    across(B + y * 64, 64)
+    across(C + z * 64, 64)
     arrived("e up 3")
     arrived("e down 2")
     e_sum[...] = piece(0)[...] + (e_up[3] + e_down[2])
     send(rows(e_sum, (1 - yhi) * 40, 40), e_last, "e y", yp(4))
-    drain(before)
-
-    for n, r in enumerate(near8):
-        arrived(("a1 y", r))
-        spread(A1 + (x * 8 + (y + NY - r) % NY) * 24, 24, "a1 x", xp, far4, True)
-        arrived(("a2 z", r))
-        spread(A2 + (x * 8 + (z + NZ - r) % NZ) * 24, 24, "a2 x", xp, far4, True)
-        if n == 3:
-            arrived("b z")
-            spread(B + y * 64, 64, "b y", yp, far8, True)
-            arrived("c y")
-            spread(C + z * 64, 64, "c z", zp, far8, True)
-    across(A1 + x * 192, 192)
+    for r in near8:
+        pass_a2(r)
     across(A2 + x * 192, 192)
-    across(B + y * 64, 64)
-    across(C + z * 64, 64)
-
     arrived("p 3")
     pred_out[...] = ((pbuf[c, x, ylo] + p3_recv[0]) + (p3_recv[1] + p3_recv[2]))[:, 0:20]
 
+    for r in near4:
+        arrived(("a1 x", r))
+        across(A1 + (x + NX - r) % NX * 192, 192)
+    arrived("e y")
+    enc_out[...] = (rows(e_sum, yhi * 40, 40)[...] + e_last[...])[:, 0:FR]
     for r in near8:
         arrived(("b y", r))
         across(B + (y + NY - r) % NY * 64, 64)
         arrived(("c z", r))
         across(C + (z + NZ - r) % NZ * 64, 64)
     for r in near4:
-        arrived(("a1 x", r))
-        across(A1 + (x + NX - r) % NX * 192, 192)
         arrived(("a2 x", r))
         across(A2 + (x + NX - r) % NX * 192, 192)
-    arrived("e y")
-    enc_out[...] = (rows(e_sum, yhi * 40, 40)[...] + e_last[...])[:, 0:FR]
     arrived("core")
 
     drain(list(index))
@@ -471,9 +471,9 @@
             vm(FR, 128), vm(FR, 128),
             vm(8, V), vm(HALF + 8, 128), vm(HALF + 8, 128), vm(HALF + 8, 128), vm(8, 72, 128),
             vm(3, 192, 128), vm(8, 72, 128), vm(3, 192, 128), vm(7, 64, 128),
-            vm(192, 128), vm(192, 128), vm(64, 128), vm(8, 16, 128),
-            vm(7, 24, 128), vm(8, 16, 128), vm(7, 24, 128), vm(7, 8, 128),
-            vm(8, 24, 128), vm(4, 16, 128), vm(8, 24, 128), vm(4, 8, 128),
+            vm(192, 128), vm(192, 128), vm(64, 128), vm(4, 24, 128),
+            vm(7, 24, 128), vm(4, 24, 128), vm(7, 24, 128), vm(3, 16, 128),
+            vm(8, 24, 128), vm(8, 24, 128), vm(8, 24, 128), vm(8, 16, 128),
             vm(128, H), vm(H, 128), vm(4, 80, 128), vm(3, 80, 128), vm(80, 128), vm(40, 128),
             vm(LB, 768), vm(2, 4, 4, LB, 128), vm(4, 4, LB, 128), vm(3, 4, LB, 128), vm(3, LB, 128),
             pltpu.SemaphoreType.DMA((SEMS,)), pltpu.SemaphoreType.DMA((SEMS,)),

time: 64.7 us -> 64.1 us (level)
  no operation moved by 1% of the time
where the time goes in v4:
time: 64.1 us; the launch traced here: 64 us
  Pallas kernels  62.7 us (98%)
  between operations  1.29 us (2%)
    pallas_call x1, Pallas kernels, local(): pl.pallas_call(kernel, out_shape=(vm(2 * HALF, 128), vm(8, 128), vm(40, F...  61.1 us
    pallas_call x1, Pallas kernels, local(): pl.pallas_call(finish, out_shape=(jax.ShapeDtypeStruct((H, V), F32), jax....  1.58 us

profile of v4, /device:TPU:1, one launch (start us, length us, event | category | flops | bytes accessed | tf_op | source)
XLA Modules:
  0.0 64.0 jit_solution(13851589914028645610)
XLA Ops:
  1.3 61.1 %joint_backward.1 = (f32[5120,128]{1,0:T(8,128)S(1)}, f32[8,128]{1,0:T(8,128)S(1)}, f32[40,96]{1,0:T(8,128)S(1)}, f32[16,20]{1,0:T(8,128)S(1)}) custom-call(bf16[96,640]{1,0:T(8,128)(2,1)} %enc_in.1, bf16[16,640]{1,0:T(8,128)(2,1)} %pred_in.1, bf16[640,1024]{1,0:T(8,128)(2,1)} %w_in.1, f32[1,1024]{1,0:T(1,128)} %bitcast.7, s32[16]{0:T(128)} %labels_in.1, ...), custom_call_target="tpu_custom_call" | custom-call | tf_op jit(solution)/shard_map/joint_backward/pallas_call | solution.py:460
  62.4 1.6 %finish.1 = (f32[640,1024]{1,0:T(8,128)}, f32[8,128]{1,0:T(8,128)}, f32[40,96]{1,0:T(8,128)}, f32[16,20]{1,0:T(8,128)}) custom-call(f32[5120,128]{1,0:T(8,128)S(1)} %get-tuple-element.12.weight, f32[8,128]{1,0:T(8,128)S(1)} %get-tuple-element.13.bias, f32[40,96]{1,0:T(8,128)S(1)} %get-tuple-element.14.enc, f32[16,20]{1,0:T(8,128)S(1)} %get-tuple-element.15.pred), custom_call_target="tpu_custom_call" | custom-call | tf_op jit(solution)/shard_map/finish/pallas_call | solution.py:490

commit v5 on v4

--- a/solution.py
+++ b/solution.py
@@ -209,14 +209,14 @@
 
     for q in range(2):
         product(other, q, peer_half)
+        for start, size in ((0, 768), (768, 512)):
+            part = q * 1280 + start
+            send(rows(peer_half, part, size), rows(core_recv, part, size), ("half", part), sibling)
         if q == 0:
             for k in range(8):
                 peer_half[HALF + k:HALF + k + 1] = jnp.sum(bias_acc[:, k * 128:(k + 1) * 128], axis=0, keepdims=True)
             acc[HALF:HALF + 8] = peer_half[HALF:HALF + 8]
             send(rows(peer_half, HALF, 8), rows(core_recv, HALF, 8), "bias", sibling)
-        for start, size in ((0, 768), (768, 512)):
-            part = q * 1280 + start
-            send(rows(peer_half, part, size), rows(core_recv, part, size), ("half", part), sibling)
     product(c, 0, acc)
 
     arrived(("half", A1))

time: 64.1 us -> 64.5 us (level)
  no operation moved by 1% of the time
where the time goes in v5:
time: 64.5 us; the launch traced here: 64.3 us
  Pallas kernels  63 us (98%)
  between operations  1.29 us (2%)
    pallas_call x1, Pallas kernels, local(): pl.pallas_call(kernel, out_shape=(vm(2 * HALF, 128), vm(8, 128), vm(40, F...  61.5 us
    pallas_call x1, Pallas kernels, local(): pl.pallas_call(finish, out_shape=(jax.ShapeDtypeStruct((H, V), F32), jax....  1.58 us

profile of v5, /device:TPU:1, one launch (start us, length us, event | category | flops | bytes accessed | tf_op | source)
XLA Modules:
  0.0 64.3 jit_solution(16265894576598454446)
XLA Ops:
  1.3 61.5 %joint_backward.1 = (f32[5120,128]{1,0:T(8,128)S(1)}, f32[8,128]{1,0:T(8,128)S(1)}, f32[40,96]{1,0:T(8,128)S(1)}, f32[16,20]{1,0:T(8,128)S(1)}) custom-call(bf16[96,640]{1,0:T(8,128)(2,1)} %enc_in.1, bf16[16,640]{1,0:T(8,128)(2,1)} %pred_in.1, bf16[640,1024]{1,0:T(8,128)(2,1)} %w_in.1, f32[1,1024]{1,0:T(1,128)} %bitcast.7, s32[16]{0:T(128)} %labels_in.1, ...), custom_call_target="tpu_custom_call" | custom-call | tf_op jit(solution)/shard_map/joint_backward/pallas_call | solution.py:460
  62.8 1.6 %finish.1 = (f32[640,1024]{1,0:T(8,128)}, f32[8,128]{1,0:T(8,128)}, f32[40,96]{1,0:T(8,128)}, f32[16,20]{1,0:T(8,128)}) custom-call(f32[5120,128]{1,0:T(8,128)S(1)} %get-tuple-element.12.weight, f32[8,128]{1,0:T(8,128)S(1)} %get-tuple-element.13.bias, f32[40,96]{1,0:T(8,128)S(1)} %get-tuple-element.14.enc, f32[16,20]{1,0:T(8,128)S(1)} %get-tuple-element.15.pred), custom_call_target="tpu_custom_call" | custom-call | tf_op jit(solution)/shard_map/finish/pallas_call | solution.py:490
